TPU v7x, 32 devices: a whole 2x2x4 slice. The times are simulated.
32 devices in a mesh: items: 8 (over z, x), rays: 4 (over y, core).
Axes of the slice: x: 2, y: 2, z: 4, core: 2. Of those that a mesh axis runs over, the one named last changes fastest.
Arguments:
- rays: bfloat16 [8, 4096, 768], P('items', 'rays'), may hold values from -6 to 6
- latents: bfloat16 [8, 1152, 768], P('items', 'rays'), may hold values from -6 to 6
- ray_scene: int32 [8, 4096], P('items', 'rays'), may hold values from 0 to 3
- latent_scene: int32 [8, 1152], P('items'), may hold values from 0 to 3, as said below
- latent_pad: int32 [8, 1152], P('items'), may hold values from 0 to 1, as said below
- cotangent: bfloat16 [8, 4096, 768], P('items', 'rays'), may hold values from -6 to 6
- query_weight: bfloat16 [768, 768], replicated, may hold values from -0.21875 to 0.21875
- key_weight: bfloat16 [768, 768], replicated, may hold values from -0.21875 to 0.21875
- value_weight: bfloat16 [768, 768], replicated, may hold values from -0.21875 to 0.21875
- out_weight: bfloat16 [768, 768], replicated, may hold values from -3 to 3
- out_bias: float32 [768], replicated, may hold values from -3 to 3
- up_weight: bfloat16 [768, 1536], replicated, may hold values from -0.21875 to 0.21875
- up_bias: float32 [1536], replicated, may hold values from -3 to 3
- down_weight: bfloat16 [1536, 768], replicated, may hold values from -0.15625 to 0.15625
- down_bias: float32 [768], replicated, may hold values from -3 to 3
- ray_gain: float32 [768], replicated, may hold values from 0.25 to 1.75
- ray_shift: float32 [768], replicated, may hold values from -3 to 3
- latent_gain: float32 [768], replicated, may hold values from 0.25 to 1.75
- latent_shift: float32 [768], replicated, may hold values from -3 to 3
- mlp_gain: float32 [768], replicated, may hold values from 0.25 to 1.75
- mlp_shift: float32 [768], replicated, may hold values from -3 to 3
Outputs:
- ray_out: bfloat16 [8, 4096, 768], P('items', 'rays')
- ray_grad: bfloat16 [8, 4096, 768], P('items', 'rays')
- latent_grad: bfloat16 [8, 1152, 768], P('items', 'rays')
- query_grad: float32 [768, 768], replicated
- key_grad: float32 [768, 768], replicated
- value_grad: float32 [768, 768], replicated
- out_grad: float32 [768, 768], replicated
- out_bias_grad: float32 [768], replicated
- up_grad: float32 [768, 1536], replicated
- up_bias_grad: float32 [1536], replicated
- down_grad: float32 [1536, 768], replicated
- down_bias_grad: float32 [768], replicated
- ray_gain_grad: float32 [768], replicated
- ray_shift_grad: float32 [768], replicated
- latent_gain_grad: float32 [768], replicated
- latent_shift_grad: float32 [768], replicated
- mlp_gain_grad: float32 [768], replicated
- mlp_shift_grad: float32 [768], replicated
Inputs may be any that keep to these rules, and one draw needn't show every extreme that they name: `latent_scene`: along each item's 1152 latent tokens the scene number never falls, and each of the 4 scenes has one or more unpadded tokens. `latent_pad`: padding tokens, one or more in each item, are the last of the item's latent tokens.
All inputs are finite; a program needn't handle non-finite values.
Results may differ from a plain program's by a relative error of at most 0.012.
The roundings to bfloat16 on the way count: a program that leaves them out, or rounds other values in their place, can miss the bound.
Values may be sent and summed in bfloat16 or wider, within the bound.
A program may use at most 256 MiB of HBM per device.

v0:
```python
import jax
import jax.numpy as jnp
from jax import lax
from jax.sharding import PartitionSpec as P

HEADS = 12
HEAD_DIM = 64


EPSILON = 1e-05
MASKED = -1000000000.0
HIGHEST = lax.Precision.HIGHEST


def norm_parts(inputs):
    center = inputs - jnp.mean(inputs, axis=-1, keepdims=True)
    inverse = lax.rsqrt(jnp.mean(center * center, axis=-1, keepdims=True) + EPSILON)
    return (center * inverse, inverse)


def norm_back(grad_out, standard, inverse, norm_gain):
    scaled = grad_out * norm_gain
    return inverse * (
        scaled
        - jnp.mean(scaled, axis=-1, keepdims=True)
        - standard * jnp.mean(scaled * standard, axis=-1, keepdims=True)
    )


def head_split(matrix):
    return matrix.reshape(matrix.shape[0], HEADS, HEAD_DIM)


def masked_scores(query_block, key_item, block_ids, latent_ids, pad_flags):
    allowed = (block_ids[:, None] == latent_ids[None, :]) & (pad_flags[None, :] == 0)
    scores = jnp.einsum(
        "rhd,lhd->hrl",
        head_split(query_block),
        head_split(key_item),
        preferred_element_type=jnp.float32,
    ) * HEAD_DIM ** (-0.5)
    return jnp.where(allowed[None], scores, MASKED)


def attend_item(inputs):
    query_item, ray_ids, pair_item, latent_ids, pad_flags = inputs
    model_width = query_item.shape[-1]
    key_item = pair_item[:, :model_width]
    value_item = pair_item[:, model_width : 2 * model_width]
    block_rows = min(512, query_item.shape[0])
    block_count = query_item.shape[0] // block_rows

    def attend_block(block_inputs):
        query_block, block_ids = block_inputs
        scores = masked_scores(query_block, key_item, block_ids, latent_ids, pad_flags)
        row_max = jnp.max(scores, axis=-1, keepdims=True)
        lifted = jnp.exp(scores - row_max)
        row_sum = jnp.sum(lifted, axis=-1, keepdims=True)
        softmax_rows = (lifted / row_sum).astype(jnp.bfloat16)
        mixture = jnp.einsum(
            "hrl,lhd->rhd", softmax_rows, head_split(value_item), preferred_element_type=jnp.float32
        )
        return (
            mixture.reshape(block_rows, model_width).astype(jnp.bfloat16),
            row_max + jnp.log(row_sum),
        )

    mixture, log_total = lax.map(
        attend_block,
        (
            query_item.reshape(block_count, block_rows, model_width),
            ray_ids.reshape(block_count, block_rows),
        ),
    )
    return (mixture.reshape(-1, model_width), log_total)


def attend_back(inputs):
    query_item, ray_ids, pair_item, latent_ids, pad_flags, grad_item, log_item = inputs
    model_width = query_item.shape[-1]
    key_item = pair_item[:, :model_width]
    value_item = pair_item[:, model_width : 2 * model_width]
    block_rows = min(512, query_item.shape[0])
    block_count = query_item.shape[0] // block_rows
    score_scale = HEAD_DIM ** (-0.5)

    def back_block(running, block_inputs):
        query_block, block_ids, grad_block, log_block = block_inputs
        scores = masked_scores(query_block, key_item, block_ids, latent_ids, pad_flags)
        softmax_full = jnp.exp(scores - log_block)
        grad_heads = head_split(grad_block)
        grad_soft = jnp.einsum(
            "rhd,lhd->hrl", grad_heads, head_split(value_item), preferred_element_type=jnp.float32
        )
        inner_sum = jnp.sum(softmax_full * grad_soft, axis=-1, keepdims=True)
        grad_scores = (softmax_full * (grad_soft - inner_sum)).astype(jnp.bfloat16)
        grad_query = (
            jnp.einsum(
                "hrl,lhd->rhd",
                grad_scores,
                head_split(key_item),
                preferred_element_type=jnp.float32,
            )
            * score_scale
        )
        grad_key = (
            jnp.einsum(
                "hrl,rhd->lhd",
                grad_scores,
                head_split(query_block),
                preferred_element_type=jnp.float32,
            )
            * score_scale
        )
        grad_value = jnp.einsum(
            "hrl,rhd->lhd",
            softmax_full.astype(jnp.bfloat16),
            grad_heads,
            preferred_element_type=jnp.float32,
        )
        key_total, value_total = running
        running = (
            key_total + grad_key.reshape(-1, model_width),
            value_total + grad_value.reshape(-1, model_width),
        )
        return (running, grad_query.reshape(block_rows, model_width).astype(jnp.bfloat16))

    empty = jnp.zeros((key_item.shape[0], model_width), jnp.float32)
    running, grad_queries = lax.scan(
        back_block,
        (empty, empty),
        (
            query_item.reshape(block_count, block_rows, model_width),
            ray_ids.reshape(block_count, block_rows),
            grad_item.reshape(block_count, block_rows, model_width),
            log_item,
        ),
    )
    return (grad_queries.reshape(-1, model_width), jnp.concatenate(running, axis=-1))


def on_device(
    rays,
    latents,
    ray_scene,
    latent_scene,
    latent_pad,
    cotangent,
    query_weight,
    key_weight,
    value_weight,
    out_weight,
    out_bias,
    up_weight,
    up_bias,
    down_weight,
    down_bias,
    ray_gain,
    ray_shift,
    latent_gain,
    latent_shift,
    mlp_gain,
    mlp_shift,
):
    item_count, ray_count, model_width = rays.shape
    pair_weight = jnp.concatenate([key_weight, value_weight], axis=1)
    ray_rows = rays.reshape(-1, model_width).astype(jnp.float32)
    ray_std, ray_inv = norm_parts(ray_rows)
    ray_normed = (ray_std * ray_gain + ray_shift).astype(jnp.bfloat16)
    queries = jnp.dot(ray_normed, query_weight, preferred_element_type=jnp.float32).astype(
        jnp.bfloat16
    )
    piece_std = norm_parts(lax.all_gather(latents, "rays", axis=1, tiled=True).astype(jnp.float32))[
        0
    ]
    piece_normed = (piece_std * latent_gain + latent_shift).astype(jnp.bfloat16)
    projected = jnp.einsum(
        "ild,de->ile", piece_normed, pair_weight, preferred_element_type=jnp.float32
    ).astype(jnp.bfloat16)
    query_items = queries.reshape(item_count, ray_count, model_width)
    mixture, log_total = lax.map(
        attend_item, (query_items, ray_scene, projected, latent_scene, latent_pad)
    )
    mixture = mixture.reshape(-1, model_width)
    hidden = ray_rows + jnp.dot(mixture, out_weight, preferred_element_type=jnp.float32) + out_bias
    mlp_std, mlp_inv = norm_parts(hidden)
    mlp_normed = (mlp_std * mlp_gain + mlp_shift).astype(jnp.bfloat16)
    pre_act = jnp.dot(mlp_normed, up_weight, preferred_element_type=jnp.float32) + up_bias
    activated, gelu_pull = jax.vjp(jax.nn.gelu, pre_act)
    activated = activated.astype(jnp.bfloat16)
    ray_out = (
        (hidden + jnp.dot(activated, down_weight, preferred_element_type=jnp.float32) + down_bias)
        .astype(jnp.bfloat16)
        .reshape(rays.shape)
    )
    upstream = cotangent.reshape(-1, model_width)
    upstream_wide = upstream.astype(jnp.float32)
    down_grad = jnp.dot(activated.T, upstream, preferred_element_type=jnp.float32)
    down_bias_grad = jnp.sum(upstream_wide, axis=0)
    grad_pre = gelu_pull(jnp.dot(upstream, down_weight.T, preferred_element_type=jnp.float32))[
        0
    ].astype(jnp.bfloat16)
    up_grad = jnp.dot(mlp_normed.T, grad_pre, preferred_element_type=jnp.float32)
    up_bias_grad = jnp.sum(grad_pre.astype(jnp.float32), axis=0)
    grad_mlp = jnp.dot(grad_pre, up_weight.T, preferred_element_type=jnp.float32)
    mlp_gain_grad = jnp.sum(grad_mlp * mlp_std, axis=0)
    mlp_shift_grad = jnp.sum(grad_mlp, axis=0)
    grad_hidden = upstream_wide + norm_back(grad_mlp, mlp_std, mlp_inv, mlp_gain)
    grad_branch = grad_hidden.astype(jnp.bfloat16)
    out_grad = jnp.dot(mixture.T, grad_branch, preferred_element_type=jnp.float32)
    out_bias_grad = jnp.sum(grad_branch.astype(jnp.float32), axis=0)
    grad_mixture = jnp.dot(grad_branch, out_weight.T, preferred_element_type=jnp.float32).astype(
        jnp.bfloat16
    )
    grad_queries, pair_grads = lax.map(
        attend_back,
        (
            query_items,
            ray_scene,
            projected,
            latent_scene,
            latent_pad,
            grad_mixture.reshape(item_count, ray_count, model_width),
            log_total,
        ),
    )
    pair_weight_wide = pair_weight.astype(jnp.float32)
    latent_rows = latents.reshape(-1, model_width).astype(jnp.float32)
    latent_std, latent_inv = norm_parts(latent_rows)
    pair_own = lax.psum_scatter(pair_grads, "rays", scatter_dimension=1, tiled=True)
    latent_normed = (
        (latent_std * latent_gain + latent_shift).astype(jnp.bfloat16).astype(jnp.float32)
    )
    pair_flat = pair_own.reshape(-1, 2 * model_width)
    pair_weight_grad = jnp.dot(
        latent_normed.T, pair_flat, precision=HIGHEST, preferred_element_type=jnp.float32
    )
    grad_latent_normed = jnp.dot(
        pair_flat, pair_weight_wide.T, precision=HIGHEST, preferred_element_type=jnp.float32
    )
    key_grad = pair_weight_grad[:, :model_width]
    value_grad = pair_weight_grad[:, model_width:]
    latent_gain_grad = jnp.sum(grad_latent_normed * latent_std, axis=0)
    latent_shift_grad = jnp.sum(grad_latent_normed, axis=0)
    latent_grad = (
        norm_back(grad_latent_normed, latent_std, latent_inv, latent_gain)
        .astype(jnp.bfloat16)
        .reshape(latents.shape)
    )
    query_flat = grad_queries.reshape(-1, model_width)
    query_grad = jnp.dot(ray_normed.T, query_flat, preferred_element_type=jnp.float32)
    grad_ray_normed = jnp.dot(query_flat, query_weight.T, preferred_element_type=jnp.float32)
    ray_gain_grad = jnp.sum(grad_ray_normed * ray_std, axis=0)
    ray_shift_grad = jnp.sum(grad_ray_normed, axis=0)
    ray_grad = (
        (grad_hidden + norm_back(grad_ray_normed, ray_std, ray_inv, ray_gain))
        .astype(jnp.bfloat16)
        .reshape(rays.shape)
    )
    summed = lax.psum(
        (
            query_grad,
            key_grad,
            value_grad,
            out_grad,
            out_bias_grad,
            up_grad,
            up_bias_grad,
            down_grad,
            down_bias_grad,
            ray_gain_grad,
            ray_shift_grad,
            latent_gain_grad,
            latent_shift_grad,
            mlp_gain_grad,
            mlp_shift_grad,
        ),
        ("items", "rays"),
    )
    return (
        ray_out,
        ray_grad,
        latent_grad,
        summed[0],
        summed[1],
        summed[2],
        summed[3],
        summed[4],
        summed[5],
        summed[6],
        summed[7],
        summed[8],
        summed[9],
        summed[10],
        summed[11],
        summed[12],
        summed[13],
        summed[14],
    )


def solution(mesh):
    in_specs = (
        P("items", "rays", None),
        P("items", "rays", None),
        P("items", "rays"),
        P("items", None),
        P("items", None),
        P("items", "rays", None),
        P(),
        P(),
        P(),
        P(),
        P(),
        P(),
        P(),
        P(),
        P(),
        P(),
        P(),
        P(),
        P(),
        P(),
        P(),
    )
    out_specs = (
        P("items", "rays", None),
        P("items", "rays", None),
        P("items", "rays", None),
        P(),
        P(),
        P(),
        P(),
        P(),
        P(),
        P(),
        P(),
        P(),
        P(),
        P(),
        P(),
        P(),
        P(),
        P(),
    )
    return jax.shard_map(
        on_device, mesh=mesh, in_specs=in_specs, out_specs=out_specs, check_vma=False
    )
```

profile of v0, /device:TPU:0, one launch (start us, length us, event | category | flops | bytes accessed | tf_op | source)
XLA Modules:
  0.0 890.8 jit_solution(13367862125813330027)
XLA Ops:
  29.3 3.8 all-gather.2.cloned.1.call-done
  37.2 5.2 convolution_convert_fusion
  44.4 3.9 copy.76
  48.3 3.9 copy.75
  53.4 87.5 %while.46 = (s32[]{:T(128)}, bf16[2,512,768]{2,1,0:T(8,128)(2,1)}, f32[2,12,512,1]{2,1,3,0:T(8,128)S(1)}, s32[2,512]{1,0:T(2,128)S(1)}, s32[1152]{0:T(1024)S(1)}...) while((s32[]{:T(128)}, bf16[2,512,768]{2,1,0:T(8,128)(2,1)}, ...), condition=%wide.region_7.8_spmd, body=%wide.region_4.7_spmd.sunk | while | flops 1898441856 | bytes 111519144 | solution.py:68
  55.4 12.0 %fusion.158 = (f32[12,512]{1,0:T(8,128)S(1)}, f32[12,512,1152]{2,1,0:T(8,128)}) fusion(pred[512,1152]{1,0:T(8,128)(4,1)S(1)} %compare_and_fusion.4, bf16[512,12,64]{0,2,1:T(8,128)(2,1)S(1)} %bitcast.224, bf16[1152,12,64]{0,2,1:T(8,128)(2,1)S(1)} %bitcast.217), kind=kOutput, calls=%fused_computation.3.clone.1 | convolution fusion | flops 927197184 | bytes 31481856 | tf_op jit(solution)/shard_map/while/body/eval_jaxpr/while/body/eval_jaxpr/rhd,lhd->hrl/dot_general | solution.py:36
  67.5 13.5 %fusion.159 = f32[12,512]{1,0:T(8,128)S(1)} fusion(f32[12,512,1152]{2,1,0:T(8,128)} %get-tuple-element.558, f32[12,512]{1,0:T(8,128)S(1)} %get-tuple-element.559, pred[512,1152]{1,0:T(8,128)(4,1)S(1)} %compare_and_fusion.4), kind=kLoop, calls=%fused_computation.4.clone.1 | loop fusion | flops 28305408 | bytes 28950528 | tf_op jit(solution)/shard_map/while/body/eval_jaxpr/while/body/eval_jaxpr/reduce_sum | solution.py:58
  81.0 14.0 %fusion.160 = bf16[12,512,64]{1,2,0:T(8,128)(2,1)} fusion(bf16[1152,12,64]{0,2,1:T(8,128)(2,1)S(1)} %bitcast.225, f32[12,512,1152]{2,1,0:T(8,128)} %get-tuple-element.558, f32[12,512]{1,0:T(8,128)S(1)} %fusion.159, f32[12,512]{1,0:T(8,128)S(1)} %get-tuple-element.559, pred[512,1152]{1,0:T(8,128)(4,1)S(1)} %compare_and_fusion.4), kind=kOutput, calls=%fused_computation.7.clone.1 | convolution fusion | flops 941752320 | bytes 31506432 | tf_op jit(solution)/shard_map/while/body/eval_jaxpr/while/body/eval_jaxpr/hrl,lhd->rhd/dot_general | solution.py:60
  99.0 12.0 %fusion.158 = (f32[12,512]{1,0:T(8,128)S(1)}, f32[12,512,1152]{2,1,0:T(8,128)}) fusion(pred[512,1152]{1,0:T(8,128)(4,1)S(1)} %compare_and_fusion.4, bf16[512,12,64]{0,2,1:T(8,128)(2,1)S(1)} %bitcast.224, bf16[1152,12,64]{0,2,1:T(8,128)(2,1)S(1)} %bitcast.217), kind=kOutput, calls=%fused_computation.3.clone.1 | convolution fusion | flops 927197184 | bytes 31481856 | tf_op jit(solution)/shard_map/while/body/eval_jaxpr/while/body/eval_jaxpr/rhd,lhd->hrl/dot_general | solution.py:36
  111.1 13.5 %fusion.159 = f32[12,512]{1,0:T(8,128)S(1)} fusion(f32[12,512,1152]{2,1,0:T(8,128)} %get-tuple-element.558, f32[12,512]{1,0:T(8,128)S(1)} %get-tuple-element.559, pred[512,1152]{1,0:T(8,128)(4,1)S(1)} %compare_and_fusion.4), kind=kLoop, calls=%fused_computation.4.clone.1 | loop fusion | flops 28305408 | bytes 28950528 | tf_op jit(solution)/shard_map/while/body/eval_jaxpr/while/body/eval_jaxpr/reduce_sum | solution.py:58
  124.6 14.0 %fusion.160 = bf16[12,512,64]{1,2,0:T(8,128)(2,1)} fusion(bf16[1152,12,64]{0,2,1:T(8,128)(2,1)S(1)} %bitcast.225, f32[12,512,1152]{2,1,0:T(8,128)} %get-tuple-element.558, f32[12,512]{1,0:T(8,128)S(1)} %fusion.159, f32[12,512]{1,0:T(8,128)S(1)} %get-tuple-element.559, pred[512,1152]{1,0:T(8,128)(4,1)S(1)} %compare_and_fusion.4), kind=kOutput, calls=%fused_computation.7.clone.1 | convolution fusion | flops 941752320 | bytes 31506432 | tf_op jit(solution)/shard_map/while/body/eval_jaxpr/while/body/eval_jaxpr/hrl,lhd->rhd/dot_general | solution.py:60
  140.9 3.9 fusion.105
  150.8 7.9 convert_reduce_fusion
  158.7 5.0 fusion.107
  167.2 4.6 multiply_reduce_fusion.1
  171.9 3.9 convert_reduce_fusion.4
  179.7 210.9 %while.47 = (s32[]{:T(128)}, f32[1152,768]{0,1:T(8,128)}, f32[1152,768]{0,1:T(8,128)}, bf16[2,512,768]{2,1,0:T(8,128)(2,1)}, bf16[2,512,768]{1,2,0:T(8,128)(2,1)...) while((s32[]{:T(128)}, f32[1152,768]{0,1:T(8,128)}, ...), condition=%wide.region_14.15_spmd.clone, body=%wide.region_12.14_spmd.clone.sunk | while | flops 4599933952 | bytes 317269632 | solution.py:129
  185.9 13.2 %fusion.171 = f32[12,512,1152]{2,1,0:T(8,128)} fusion(bf16[512,12,64]{0,2,1:T(8,128)(2,1)S(1)} %bitcast.220, bf16[1152,12,64]{0,2,1:T(8,128)(2,1)} %bitcast.226), kind=kOutput, calls=%fused_computation.170.clone.1 | convolution fusion | flops 905969664 | bytes 30867456 | tf_op jit(solution)/shard_map/while/body/eval_jaxpr/while/body/eval_jaxpr/rhd,lhd->hrl/dot_general | solution.py:92
  199.1 21.6 %multiply_reduce_fusion.8 = (f32[12,512]{1,0:T(8,128)S(1)}, f32[12,512,1152]{2,1,0:T(8,128)}) fusion(f32[12,512,1152]{2,1,0:T(8,128)} %fusion.171, f32[12,512]{1,0:T(8,128)S(1)} %dynamic-slice_bitcast_fusion.2, bf16[512,12,64]{0,2,1:T(8,128)(2,1)S(1)} %bitcast.222, bf16[1152,12,64]{0,2,1:T(8,128)(2,1)S(1)} %bitcast.219, ...), kind=kOutput, calls=%fused_computation.16.clone.1 | convolution fusion | flops 941352960 | bytes 59817984 | tf_op jit(solution)/shard_map/while/body/eval_jaxpr/while/body/eval_jaxpr/rhd,lhd->hrl/dot_general | solution.py:36
  220.6 23.4 %multiply_convert_fusion.7 = bf16[12,512,1152]{2,1,0:T(8,128)(2,1)} fusion(f32[12,512,1152]{2,1,0:T(8,128)} %get-tuple-element.572, f32[12,512,1152]{2,1,0:T(8,128)} %fusion.171, f32[12,512]{1,0:T(8,128)S(1)} %get-tuple-element.573), kind=kLoop, calls=%fused_computation.15.clone.1 | loop fusion | flops 21233664 | bytes 70803456 | tf_op jit(solution)/shard_map/while/body/eval_jaxpr/while/body/eval_jaxpr/convert_element_type | solution.py:96
  244.0 13.4 %fusion.172 = f32[12,64,1152]{2,1,0:T(8,128)} fusion(bf16[512,12,64]{0,2,1:T(8,128)(2,1)S(1)} %bitcast.221, f32[12,512,1152]{2,1,0:T(8,128)} %get-tuple-element.572), kind=kOutput, calls=%fused_computation.18.clone.1 | convolution fusion | flops 913047552 | bytes 32636928 | tf_op jit(solution)/shard_map/while/body/eval_jaxpr/while/body/eval_jaxpr/hrl,rhd->lhd/dot_general | solution.py:115
  257.5 10.8 %multiply_convert_fusion.8 = bf16[12,512,64]{1,2,0:T(8,128)(2,1)} fusion(bf16[12,512,1152]{2,1,0:T(8,128)(2,1)} %multiply_convert_fusion.7, bf16[1152,12,64]{0,2,1:T(8,128)(2,1)} %bitcast.218), kind=kOutput, calls=%fused_computation.24.clone.1 | convolution fusion | flops 906756096 | bytes 16711680 | tf_op jit(solution)/shard_map/while/body/eval_jaxpr/while/body/eval_jaxpr/hrl,lhd->rhd/dot_general | solution.py:98
  268.3 7.7 convolution_multiply_fusion.2
  276.1 4.0 bitcast_add_fusion.3
  290.2 13.2 %fusion.171 = f32[12,512,1152]{2,1,0:T(8,128)} fusion(bf16[512,12,64]{0,2,1:T(8,128)(2,1)S(1)} %bitcast.220, bf16[1152,12,64]{0,2,1:T(8,128)(2,1)} %bitcast.226), kind=kOutput, calls=%fused_computation.170.clone.1 | convolution fusion | flops 905969664 | bytes 30867456 | tf_op jit(solution)/shard_map/while/body/eval_jaxpr/while/body/eval_jaxpr/rhd,lhd->hrl/dot_general | solution.py:92
  303.3 21.6 %multiply_reduce_fusion.8 = (f32[12,512]{1,0:T(8,128)S(1)}, f32[12,512,1152]{2,1,0:T(8,128)}) fusion(f32[12,512,1152]{2,1,0:T(8,128)} %fusion.171, f32[12,512]{1,0:T(8,128)S(1)} %dynamic-slice_bitcast_fusion.2, bf16[512,12,64]{0,2,1:T(8,128)(2,1)S(1)} %bitcast.222, bf16[1152,12,64]{0,2,1:T(8,128)(2,1)S(1)} %bitcast.219, ...), kind=kOutput, calls=%fused_computation.16.clone.1 | convolution fusion | flops 941352960 | bytes 59817984 | tf_op jit(solution)/shard_map/while/body/eval_jaxpr/while/body/eval_jaxpr/rhd,lhd->hrl/dot_general | solution.py:36
  324.9 23.4 %multiply_convert_fusion.7 = bf16[12,512,1152]{2,1,0:T(8,128)(2,1)} fusion(f32[12,512,1152]{2,1,0:T(8,128)} %get-tuple-element.572, f32[12,512,1152]{2,1,0:T(8,128)} %fusion.171, f32[12,512]{1,0:T(8,128)S(1)} %get-tuple-element.573), kind=kLoop, calls=%fused_computation.15.clone.1 | loop fusion | flops 21233664 | bytes 70803456 | tf_op jit(solution)/shard_map/while/body/eval_jaxpr/while/body/eval_jaxpr/convert_element_type | solution.py:96
  348.3 13.4 %fusion.172 = f32[12,64,1152]{2,1,0:T(8,128)} fusion(bf16[512,12,64]{0,2,1:T(8,128)(2,1)S(1)} %bitcast.221, f32[12,512,1152]{2,1,0:T(8,128)} %get-tuple-element.572), kind=kOutput, calls=%fused_computation.18.clone.1 | convolution fusion | flops 913047552 | bytes 32636928 | tf_op jit(solution)/shard_map/while/body/eval_jaxpr/while/body/eval_jaxpr/hrl,rhd->lhd/dot_general | solution.py:115
  361.7 10.8 %multiply_convert_fusion.8 = bf16[12,512,64]{1,2,0:T(8,128)(2,1)} fusion(bf16[12,512,1152]{2,1,0:T(8,128)(2,1)} %multiply_convert_fusion.7, bf16[1152,12,64]{0,2,1:T(8,128)(2,1)} %bitcast.218), kind=kOutput, calls=%fused_computation.24.clone.1 | convolution fusion | flops 906756096 | bytes 16711680 | tf_op jit(solution)/shard_map/while/body/eval_jaxpr/while/body/eval_jaxpr/hrl,lhd->rhd/dot_general | solution.py:98
  372.6 7.7 convolution_multiply_fusion.2
  380.3 6.0 bitcast_add_fusion.3
  390.6 5.2 copy.87
  395.8 5.2 copy.88
  401.0 3.9 pad_maximum_fusion
  404.9 13.4 %broadcast_in_dim.43 = f32[1,1152,1536]{2,0,1:T(1,128)} reshape(f32[1152,1536]{1,0:T(8,128)S(1)} %pad_maximum_fusion) | data formatting | bytes 14155776 | tf_op jit(solution)/shard_map/while/body/jit(dynamic_update_index_in_dim)/broadcast_in_dim | solution.py:215
  420.7 5.4 fusion.98
  429.5 4.5 fusion.101
  434.0 5.7 fusion.60
  439.8 111.0 %all-reduce.6.cloned.1.call-done = f32[1,1152,1536]{2,0,1:T(1,128)} async-done(((f32[1,1152,1536]{2,0,1:T(1,128)}), f32[1,1152,1536]{2,0,1:T(1,128)}) %all-reduce.6.cloned.1.call-update) | async-done | bytes 7077904
  553.5 4.1 fusion.45
  560.9 8.2 fusion.74
  571.7 4.9 fusion.106
  576.5 3.7 copy.86
  580.3 3.6 fusion.36
  584.3 4.2 fusion.58
  591.1 5.7 fusion.85
  596.8 42.3 %all-reduce.1 = (f32[768]{0:T(1024)}, f32[1536]{0:T(1024)}, f32[768]{0:T(1024)}, f32[768]{0:T(1024)}, f32[768]{0:T(1024)}, /*index=5*/f32[768]{0:T(1024)}, f32[768]{0:T(1024)}, f32[768]{0:T(1024)}, f32[768]{0:T(1024)}) all-reduce(f32[768]{0:T(1024)S(1)} %copy-done.47, ...), channel_id=1, replica_groups=mesh['items'=8,'rays'=4] {'items','rays'}, use_global_device_ids=true, to_apply=%region_27.28 | all-reduce | flops 7680 | bytes 61440 | tf_op jit(solution)/shard_map/psum | solution.py:260
  641.4 227.6 %all-reduce.8.cloned.1.call-done = (f32[768,768]{1,0:T(8,128)}, f32[768,768]{1,0:T(8,128)}, f32[768,768]{1,0:T(8,128)}, f32[768,768]{1,0:T(8,128)}, f32[768,1536]{1,0:T(8,128)}, /*index=5*/f32[1536,768]{1,0:T(8,128)}) async-done(((f32[768,768]{1,0:T(8,128)}, f32[768,768]{1,0:T(8,128)}, f32[768,768]{1,0:T(8,128)}, f32[768,768]{1,0:T(8,128)}, f32[768,1536]{1,0:T(8,128)}, /*index=5*/f32[1536,768]{1,0:T(8,128)}), ...) | async-done | bytes 18874384 | tf_op jit(solution)/shard_map/psum | solution.py:260
  (260 shorter events, 105.0 us)
Async XLA Ops:
  7.2 143.6 %copy-start = (bf16[1536,768]{1,0:T(8,128)(2,1)S(1)}, bf16[1536,768]{1,0:T(8,128)(2,1)}, u32[]{:S(2)}) copy-start(bf16[1536,768]{1,0:T(8,128)(2,1)} %param.38) | copy-start | bytes 7077892
  7.2 25.9 %all-gather.2.cloned.1.call-start = ((), (), s32[]{:S(2)}) async-start(), calls=%async_computation | async-start | bytes 2211840 | tf_op jit(solution)/shard_map/all_gather | solution.py:173
  7.9 542.9 %all-reduce.6.cloned.1.call-start = ((), (), s32[]{:S(2)}) async-start(), calls=%async_computation.1 | async-start | bytes 14155776
  11.9 6.4 copy-start.42
  11.9 6.3 copy-start.59
  16.4 4.9 copy-start.32
  21.2 5.3 copy-start.28
  28.2 8.9 %copy-start.44 = (f32[768]{0:T(1024)S(1)}, f32[768]{0:T(1024)}, u32[]{:S(2)}) copy-start(f32[768]{0:T(1024)} %param.42) | copy-start | bytes 9220
  28.2 8.9 %copy-start.50 = (f32[768]{0:T(1024)S(1)}, f32[768]{0:T(1024)}, u32[]{:S(2)}) copy-start(f32[768]{0:T(1024)} %param.43) | copy-start | bytes 9220
  48.3 5.1 copy-start.30
  48.3 5.1 copy-start.31
  53.4 87.5 %copy-start.58 = (f32[768]{0:T(1024)S(1)}, f32[768]{0:T(1024)}, u32[]{:S(2)}) copy-start(f32[768]{0:T(1024)} %param.35) | copy-start | bytes 9220
  67.5 13.5 %copy-start.6 = (bf16[1152,768]{0,1:T(8,128)(2,1)S(1)}, bf16[1152,768]{0,1:T(8,128)(2,1)}, u32[]{:S(2)}) copy-start(bf16[1152,768]{0,1:T(8,128)(2,1)} %get-tuple-element.604) | copy-start | bytes 5308420 | tf_op jit(solution)/shard_map/while/body/eval_jaxpr/while
  111.1 13.5 %copy-start.6 = (bf16[1152,768]{0,1:T(8,128)(2,1)S(1)}, bf16[1152,768]{0,1:T(8,128)(2,1)}, u32[]{:S(2)}) copy-start(bf16[1152,768]{0,1:T(8,128)(2,1)} %get-tuple-element.604) | copy-start | bytes 5308420 | tf_op jit(solution)/shard_map/while/body/eval_jaxpr/while
  144.9 26.9 %copy-start.34 = (f32[1024]{0:T(1024)}, f32[1024]{0:T(1024)S(1)}, u32[]{:S(2)}) copy-start(f32[1024]{0:T(1024)S(1)} %broadcast_multiply_fusion.5) | copy-start | bytes 12292
  147.7 24.1 %copy-start.38 = (f32[1024]{0:T(1024)}, f32[1024]{0:T(1024)S(1)}, u32[]{:S(2)}) copy-start(f32[1024]{0:T(1024)S(1)} %add_rsqrt_fusion.1) | copy-start | bytes 12292
  150.8 7.9 copy-start.65
  158.7 5.0 copy-start.66
  185.9 13.2 %copy-start.4 = (bf16[1,512,768]{1,2,0:T(8,128)(2,1)}, bf16[1,512,768]{1,2,0:T(8,128)(2,1)S(1)}, u32[]{:S(2)}) copy-start(bf16[1,512,768]{1,2,0:T(8,128)(2,1)S(1)} %constant_dynamic-slice_fusion.14) | copy-start | bytes 2359300 | tf_op jit(solution)/shard_map/while/body/eval_jaxpr/while
  185.9 13.2 %copy-start.2 = (bf16[1152,768]{0,1:T(8,128)(2,1)S(1)}, bf16[1152,768]{0,1:T(8,128)(2,1)}, u32[]{:S(2)}) copy-start(bf16[1152,768]{0,1:T(8,128)(2,1)} %get-tuple-element.642) | copy-start | bytes 5308420 | tf_op jit(solution)/shard_map/while/body/eval_jaxpr/while
  185.9 13.2 %copy-start.7 = (pred[512,1152]{1,0:T(8,128)(4,1)S(1)}, pred[512,1152]{1,0:T(8,128)(4,1)}, u32[]{:S(2)}) copy-start(pred[512,1152]{1,0:T(8,128)(4,1)} %compare_and_fusion.5) | copy-start | bytes 1769476 | tf_op jit(solution)/shard_map/while/body/eval_jaxpr/while
  257.4 10.9 %copy-start.5 = (bf16[1,512,768]{1,2,0:T(8,128)(2,1)S(1)}, bf16[1,512,768]{1,2,0:T(8,128)(2,1)}, u32[]{:S(2)}) copy-start(bf16[1,512,768]{1,2,0:T(8,128)(2,1)} %copy-done.4) | copy-start | bytes 2359300 | tf_op jit(solution)/shard_map/while/body/eval_jaxpr/while
  268.3 7.7 copy-start.3
  268.3 7.7 copy-start.8
  290.1 13.2 %copy-start.4 = (bf16[1,512,768]{1,2,0:T(8,128)(2,1)}, bf16[1,512,768]{1,2,0:T(8,128)(2,1)S(1)}, u32[]{:S(2)}) copy-start(bf16[1,512,768]{1,2,0:T(8,128)(2,1)S(1)} %constant_dynamic-slice_fusion.14) | copy-start | bytes 2359300 | tf_op jit(solution)/shard_map/while/body/eval_jaxpr/while
  290.2 13.2 %copy-start.2 = (bf16[1152,768]{0,1:T(8,128)(2,1)S(1)}, bf16[1152,768]{0,1:T(8,128)(2,1)}, u32[]{:S(2)}) copy-start(bf16[1152,768]{0,1:T(8,128)(2,1)} %get-tuple-element.642) | copy-start | bytes 5308420 | tf_op jit(solution)/shard_map/while/body/eval_jaxpr/while
  290.2 13.2 %copy-start.7 = (pred[512,1152]{1,0:T(8,128)(4,1)S(1)}, pred[512,1152]{1,0:T(8,128)(4,1)}, u32[]{:S(2)}) copy-start(pred[512,1152]{1,0:T(8,128)(4,1)} %compare_and_fusion.5) | copy-start | bytes 1769476 | tf_op jit(solution)/shard_map/while/body/eval_jaxpr/while
  361.7 10.9 %copy-start.5 = (bf16[1,512,768]{1,2,0:T(8,128)(2,1)S(1)}, bf16[1,512,768]{1,2,0:T(8,128)(2,1)}, u32[]{:S(2)}) copy-start(bf16[1,512,768]{1,2,0:T(8,128)(2,1)} %copy-done.4) | copy-start | bytes 2359300 | tf_op jit(solution)/shard_map/while/body/eval_jaxpr/while
  372.6 7.7 copy-start.3
  372.6 7.7 copy-start.8
  418.3 450.7 %all-reduce.8.cloned.1.call-start = ((), (), s32[]{:S(2)}) async-start(), calls=%async_computation.2 | async-start | bytes 37748736 | tf_op jit(solution)/shard_map/psum | solution.py:260
  420.6 5.4 copy-start.11
  420.6 5.4 copy-start.27
  420.6 5.4 copy-start.33
  420.6 5.4 copy-start.37
  420.7 5.4 copy-start.43
  420.7 5.4 copy-start.60
  426.2 7.8 slice-start.4
  439.8 113.7 %copy-start.45 = (f32[768]{0:T(1024)S(1)}, f32[768]{0:T(1024)}, u32[]{:S(2)}) copy-start(f32[768]{0:T(1024)} %param.42) | copy-start | bytes 9220
  439.8 113.7 %copy-start.51 = (f32[768]{0:T(1024)S(1)}, f32[768]{0:T(1024)}, u32[]{:S(2)}) copy-start(f32[768]{0:T(1024)} %param.43) | copy-start | bytes 9220
  591.0 5.7 copy-start.46
  591.0 5.7 copy-start.47
  591.0 5.7 copy-start.48
  591.0 5.7 copy-start.49
  591.0 5.7 copy-start.52
  869.0 4.8 copy-start.23
  872.4 6.0 slice-start.2
  876.9 4.8 slice-start
  (38 other events, 116.1 us)
Sparse Core Ops, SparseCore 0:
  9.6 23.4 all-gather.1
  418.4 132.3 all-reduce.5
  560.4 308.5 all-reduce.7
where the time goes:
time: 898 us; the launch traced here: 891 us
  waiting for transfers between devices  343 us (38%)
  matrix products  257 us (29%)
  other arithmetic  121 us (13%)
  local copies, waits for them, and re-layouts  111 us (12%)
  blocking collectives  42.3 us (5%)
  between operations  15.2 us (2%)
    psum x1, waiting for transfers between devices, on_device(): lax.psum((query_grad, key_grad, value_grad, out_grad, out_bias_grad, up_g...  228 us
    unnamed x4, waiting for transfers between devices  112 us
    dot_general x4, matrix products, masked_scores(): jnp.einsum('rhd,lhd->hrl', head_split(query_block), head_split(key_item),...  67.2 us
    convert_element_type x2, other arithmetic, back_block(): grad_scores = (softmax_full * (grad_soft - inner_sum)).astype(jnp.bfloat16)  46.8 us
    psum x1, blocking collectives, on_device(): lax.psum((query_grad, key_grad, value_grad, out_grad, out_bias_grad, up_g...  42.3 us
    unnamed x144, local copies, waits for them, and re-layouts  35.6 us
    dot_general x2, matrix products, attend_block(): jnp.einsum('hrl,lhd->rhd', softmax_rows, head_split(value_item), preferre...  28 us
    reduce_sum x2, other arithmetic, attend_block(): row_sum = jnp.sum(lifted, axis=-1, keepdims=True)  27 us
  transfers between devices with their start and end apart: 3, of which 3 were waited for; matrix products, arithmetic and copies ran while one was open for 9% of the time, Pallas kernels for 0%

commit v1 on v0

v1 whole, which is shorter than its diff:
```python
import functools

import jax
import jax.numpy as jnp
from jax import lax
from jax.experimental import pallas as pl
from jax.experimental.pallas import tpu as pltpu
from jax.sharding import PartitionSpec as P

HEADS = 12
HEAD_DIM = 64
PAIRS = HEADS // 2
SCENES = 4
EPSILON = 1e-05
SCALE = HEAD_DIM ** (-0.5)
BLOCK = 128
WINDOW = 256
OUTSIDE = -1e30
MESH = pl.DeviceIdType.MESH
F32 = jnp.float32
BF16 = jnp.bfloat16
MIB = 2**20


def dot(left, right, left_dim=1, right_dim=0):
    return lax.dot_general(
        left, right, (((left_dim,), (right_dim,)), ((), ())), preferred_element_type=F32
    )


def stand(rows):
    center = rows - jnp.mean(rows, axis=-1, keepdims=True)
    inverse = lax.rsqrt(jnp.mean(center * center, axis=-1, keepdims=True) + EPSILON)
    return center * inverse, inverse


def norm_back(grad_out, standard, inverse, gain):
    scaled = grad_out * gain
    return inverse * (
        scaled
        - jnp.mean(scaled, axis=-1, keepdims=True)
        - standard * jnp.mean(scaled * standard, axis=-1, keepdims=True)
    )


def vmem():
    return pl.BlockSpec(memory_space=pltpu.VMEM)


def smem():
    return pl.BlockSpec(memory_space=pltpu.SMEM)


def anywhere():
    return pl.BlockSpec(memory_space=pl.ANY)


def peer(axis, bit):
    return {axis: lax.bitwise_xor(lax.axis_index(axis), bit)}


def greet(partners):
    barrier = pltpu.get_barrier_semaphore()
    for axis, bit in partners:
        pl.semaphore_signal(barrier, inc=1, device_id=peer(axis, bit), device_id_type=MESH)
    pl.semaphore_wait(barrier, len(partners))


def project_kernel(
    rays, latents, query_w, key_w, value_w, ray_gain, ray_shift, latent_gain, latent_shift,
    ray_normed, queries, keys, values, latent_normed, latent_all,
    landed, send_sem, recv_sem,
):
    me = lax.axis_index("rays")
    lat = latents.shape[0]
    near, far = ("rays", 1), ("rays", 2)
    greet([near, far])

    def copy(src, slot, partner, index):
        return pltpu.make_async_remote_copy(
            src_ref=src,
            dst_ref=landed.at[slot],
            send_sem=send_sem.at[index],
            recv_sem=recv_sem.at[index],
            device_id=peer(*partner),
            device_id_type=MESH,
        )

    to_far = copy(latents, 1, far, 1)
    to_near = copy(latents, 0, near, 0)
    to_far.start()
    to_near.start()

    chunk = 256

    @pl.loop(0, rays.shape[0] // chunk)
    def _(i):
        rows = pl.ds(pl.multiple_of(i * chunk, chunk), chunk)
        standard, _ = stand(rays[rows, :].astype(F32))
        normed = (standard * ray_gain[...] + ray_shift[...]).astype(BF16)
        ray_normed[rows, :] = normed
        projected = dot(normed, query_w[...]).astype(BF16)
        queries[rows, :] = (projected.astype(F32) * SCALE).astype(BF16)

    def one(raw, owner):
        rows = pl.ds(pl.multiple_of(owner * lat, 32), lat)
        latent_all[rows, :] = raw
        standard, _ = stand(raw.astype(F32))
        normed = (standard * latent_gain[...] + latent_shift[...]).astype(BF16)
        latent_normed[rows, :] = normed
        keys[rows, :] = dot(normed, key_w[...]).astype(BF16)
        values[rows, :] = dot(normed, value_w[...]).astype(BF16)

    total = 4 * lat
    keys[total:, :] = jnp.zeros((keys.shape[0] - total, keys.shape[1]), BF16)
    values[total:, :] = jnp.zeros((keys.shape[0] - total, keys.shape[1]), BF16)
    one(latents[...], me)
    to_far.wait_recv()
    passed = copy(landed.at[1], 2, near, 2)
    passed.start()
    to_near.wait_recv()
    one(landed[0], lax.bitwise_xor(me, 1))
    one(landed[1], lax.bitwise_xor(me, 2))
    passed.wait_recv()
    one(landed[2], lax.bitwise_xor(me, 3))
    to_far.wait_send()
    to_near.wait_send()
    passed.wait_send()


def lanes_of(shape):
    return lax.broadcasted_iota(jnp.int32, shape, len(shape) - 1)


def sort_rows(target, source, position_row):
    count = source.shape[0]
    step = 256

    @pl.loop(0, count // step)
    def _(i):
        first = pl.multiple_of(i * step, step)
        index = lax.broadcasted_iota(jnp.int32, (step, count), 0) + first
        chosen = jnp.where(index == position_row[...], 1.0, 0.0).astype(BF16)
        target[pl.ds(first, step), :] = dot(chosen, source[...]).astype(BF16)


def unsort_rows(target, source, position_column):
    count = source.shape[0]
    step = 256

    @pl.loop(0, count // step)
    def _(i):
        first = pl.multiple_of(i * step, step)
        index = lax.broadcasted_iota(jnp.int32, (step, count), 1)
        chosen = jnp.where(index == position_column[pl.ds(first, step), :], 1.0, 0.0).astype(BF16)
        target[pl.ds(first, step), :] = dot(chosen, source[...]).astype(BF16)


def latent_features(meta, extra, with_ones):
    shape = extra.shape
    row = lax.broadcasted_iota(jnp.int32, shape, 0)
    lane = lanes_of(shape)
    first = jnp.full(shape, meta[5], jnp.int32)
    last = jnp.full(shape, meta[6], jnp.int32)
    for s in range(1, SCENES):
        first = jnp.where(lane == s, meta[5 + s], first)
        last = jnp.where(lane == s, meta[6 + s], last)
    inside = (row >= first) & (row < last)
    value = jnp.where(inside | (lane >= SCENES), 0.0, OUTSIDE)
    if with_ones:
        value = jnp.where((lane >= SCENES) & (lane < SCENES + 3), 1.0, value)
    extra[...] = value.astype(BF16)


def ray_features(meta, block):
    shape = (BLOCK, 128)
    row = lax.broadcasted_iota(jnp.int32, shape, 0) + block * BLOCK
    lane = lanes_of(shape)
    value = jnp.zeros(shape, F32)
    for s in range(SCENES):
        value = jnp.where((lane == s) & (row >= meta[s]) & (row < meta[s + 1]), 1.0, value)
    return value


def half_masks():
    lane = lanes_of((BLOCK, 128))
    low = jnp.where(lane < HEAD_DIM, 1.0, 0.0)
    return low, 1.0 - low


def pick_halves(both):
    lane = lanes_of((BLOCK, 128))
    return jnp.where(lane < HEAD_DIM, both[:BLOCK, :128], both[BLOCK:, :128])


def attend_kernel(
    meta, queries, keys, values, position_row, position_column,
    mixture, sorted_queries, sorted_mixture, log_total,
    latent_extra, stacked, total, peak,
):
    rays = queries.shape[0]
    latent_features(meta, latent_extra, False)
    sort_rows(sorted_queries, queries, position_row)
    ones = jnp.where(lanes_of((WINDOW, 128)) == 0, 1.0, 0.0).astype(BF16)
    low, high = half_masks()
    lane = lanes_of((BLOCK, 128))

    @pl.loop(0, rays // BLOCK)
    def _(block):
        rows = pl.ds(pl.multiple_of(block * BLOCK, BLOCK), BLOCK)
        extra = ray_features(meta, block).astype(BF16)
        for p in range(PAIRS):
            pair = sorted_queries[rows, 128 * p : 128 * (p + 1)].astype(F32)
            stacked[p, :BLOCK, :128] = (pair * low).astype(BF16)
            stacked[p, BLOCK:, :128] = (pair * high).astype(BF16)
            stacked[p, :BLOCK, 128:] = extra
            stacked[p, BLOCK:, 128:] = extra
            total[p] = jnp.zeros((2 * BLOCK, 256), F32)
            peak[p] = jnp.full((2 * BLOCK, 1), -3e38, F32)

        @pl.loop(0, meta[18 + block])
        def _(w):
            window = pl.ds(pl.multiple_of(meta[10 + block] + w * WINDOW, 16), WINDOW)
            extra_keys = latent_extra[window, :]
            for p in range(PAIRS):
                key_side = jnp.concatenate([keys[window, 128 * p : 128 * (p + 1)], extra_keys], axis=1)
                scores = dot(stacked[p], key_side, 1, 1)
                before = peak[p]
                now = jnp.maximum(before, jnp.max(scores, axis=1, keepdims=True))
                lifted = jnp.exp(scores - now).astype(BF16)
                value_side = jnp.concatenate([values[window, 128 * p : 128 * (p + 1)], ones], axis=1)
                total[p] = total[p] * jnp.exp(before - now) + dot(lifted, value_side)
                peak[p] = now

        logs = jnp.zeros((BLOCK, 128), F32)
        for p in range(PAIRS):
            both = total[p]
            sums = both[:, 128:129]
            mixed = pick_halves(both[:, :128] * (1.0 / sums))
            sorted_mixture[rows, 128 * p : 128 * (p + 1)] = mixed.astype(BF16)
            log_rows = peak[p] + jnp.log(sums)
            logs = jnp.where(lane == 2 * p, log_rows[:BLOCK], logs)
            logs = jnp.where(lane == 2 * p + 1, log_rows[BLOCK:], logs)
        log_total[rows, :] = logs

    unsort_rows(mixture, sorted_mixture, position_column)


def three_parts(column, first_lane):
    lane = lanes_of((BLOCK, 128))
    value = -column
    top = value.astype(BF16).astype(F32)
    rest = value - top
    middle = rest.astype(BF16).astype(F32)
    lowest = rest - middle
    out = jnp.where(lane == first_lane, top, 0.0)
    out = jnp.where(lane == first_lane + 1, middle, out)
    return jnp.where(lane == first_lane + 2, lowest, out)


def attend_back_kernel(
    meta, sorted_queries, keys, values, sorted_mixture, log_total, grad_mixture, position_row, position_column,
    grad_queries, grad_keys, grad_values,
    latent_extra, stacked, stacked_grad, sorted_grad, key_total, value_total, query_total,
):
    rays = sorted_queries.shape[0]
    latent_features(meta, latent_extra, True)
    sort_rows(sorted_grad, grad_mixture, position_row)
    ones = jnp.where(lanes_of((WINDOW, 128)) < 3, 1.0, 0.0).astype(BF16)
    low, high = half_masks()
    key_total[...] = jnp.zeros(key_total.shape, F32)
    value_total[...] = jnp.zeros(value_total.shape, F32)

    @pl.loop(0, rays // BLOCK)
    def _(block):
        rows = pl.ds(pl.multiple_of(block * BLOCK, BLOCK), BLOCK)
        extra = ray_features(meta, block)
        logs = log_total[rows, :]
        for p in range(PAIRS):
            columns = slice(128 * p, 128 * (p + 1))
            pair = sorted_queries[rows, columns].astype(F32)
            grad = sorted_grad[rows, columns].astype(F32)
            product = grad * sorted_mixture[rows, columns].astype(F32)
            for side, mask in enumerate((low, high)):
                half = slice(side * BLOCK, (side + 1) * BLOCK)
                head = 2 * p + side
                stacked[p, half, :128] = (pair * mask).astype(BF16)
                stacked[p, half, 128:] = (extra + three_parts(logs[:, head : head + 1], SCENES)).astype(BF16)
                inner = jnp.sum(product * mask, axis=1, keepdims=True)
                stacked_grad[p, half, :128] = (grad * mask).astype(BF16)
                stacked_grad[p, half, 128:] = three_parts(inner, 0).astype(BF16)
            query_total[p] = jnp.zeros((2 * BLOCK, 128), F32)

        @pl.loop(0, meta[18 + block])
        def _(w):
            window = pl.ds(pl.multiple_of(meta[10 + block] + w * WINDOW, 16), WINDOW)
            extra_keys = latent_extra[window, :]
            for p in range(PAIRS):
                columns = slice(128 * p, 128 * (p + 1))
                key_pair = keys[window, columns]
                probs = jnp.exp(dot(jnp.concatenate([key_pair, extra_keys], axis=1), stacked[p], 1, 1))
                value_side = jnp.concatenate([values[window, columns], ones], axis=1)
                centered = dot(value_side, stacked_grad[p], 1, 1)
                grad_scores = (probs * centered).astype(BF16)
                value_total[window, columns] += dot(probs.astype(BF16), stacked_grad[p, :, :128])
                key_total[window, columns] += dot(grad_scores, stacked[p, :, :128])
                query_total[p] += dot(grad_scores, key_pair, 0, 0)

        for p in range(PAIRS):
            sorted_grad[rows, 128 * p : 128 * (p + 1)] = (pick_halves(query_total[p]) * SCALE).astype(BF16)

    unsort_rows(grad_queries, sorted_grad, position_column)
    count = grad_keys.shape[0]
    grad_keys[...] = key_total[:count, :].astype(BF16)
    grad_values[...] = value_total[:count, :].astype(BF16)


def mlp_kernel(
    rays, mixture, cotangent, out_w, up_w, down_w, out_bias, up_bias, down_bias, mlp_gain, mlp_shift,
    ray_out, grad_mixture, grad_hidden, early, sums,
    act, grad_pre, normed, branch,
):
    chunk = 256
    width = rays.shape[1]
    sums[...] = jnp.zeros(sums.shape, F32)
    root = 0.7978845608028654
    cubic = 0.044715

    @pl.loop(0, rays.shape[0] // chunk)
    def _(i):
        rows = pl.ds(pl.multiple_of(i * chunk, chunk), chunk)
        hidden = rays[rows, :].astype(F32) + dot(mixture[rows, :], out_w[...]) + out_bias[...]
        standard, inverse = stand(hidden)
        low = (standard * mlp_gain[...] + mlp_shift[...]).astype(BF16)
        normed[rows, :] = low
        upstream = cotangent[rows, :]
        half = 768
        out = hidden + down_bias[...]
        grad_mlp = jnp.zeros((chunk, width), F32)
        for j in range(up_w.shape[1] // half):
            cols = slice(j * half, (j + 1) * half)
            pre = dot(low, up_w[:, cols]) + up_bias[:, cols]
            square = pre * pre
            bend = jnp.tanh(root * pre * (1.0 + cubic * square))
            rise = 0.5 * (1.0 + bend)
            active = (pre * rise).astype(BF16)
            slope = rise + 0.5 * pre * (1.0 - bend * bend) * (root * (1.0 + 3.0 * cubic * square))
            act[rows, cols] = active
            out = out + dot(active, down_w[cols, :])
            back = (dot(upstream, down_w[cols, :], 1, 1) * slope).astype(BF16)
            grad_pre[rows, cols] = back
            sums[1 + j : 2 + j, :] += jnp.sum(back.astype(F32), axis=0, keepdims=True)
            grad_mlp = grad_mlp + dot(back, up_w[:, cols], 1, 1)
        ray_out[rows, :] = out.astype(BF16)
        wide = upstream.astype(F32)
        sums[0:1, :] += jnp.sum(wide, axis=0, keepdims=True)
        sums[3:4, :] += jnp.sum(grad_mlp * standard, axis=0, keepdims=True)
        sums[4:5, :] += jnp.sum(grad_mlp, axis=0, keepdims=True)
        through = wide + norm_back(grad_mlp, standard, inverse, mlp_gain[...])
        grad_hidden[rows, :] = through
        rounded = through.astype(BF16)
        branch[rows, :] = rounded
        sums[5:6, :] += jnp.sum(rounded.astype(F32), axis=0, keepdims=True)
        grad_mixture[rows, :] = dot(rounded, out_w[...], 1, 1).astype(BF16)

    step = 256

    @pl.loop(0, down_w.shape[0] // step)
    def _(j):
        cols = pl.ds(pl.multiple_of(j * step, step), step)
        early[cols, :] = dot(act[:, cols], cotangent[...], 0, 0).astype(BF16)

    @pl.loop(0, width // step)
    def _(j):
        first = pl.multiple_of(j * step, step)
        cols = pl.ds(first, step)
        for h in range(2):
            part = dot(normed[:, cols], grad_pre[:, h * width : (h + 1) * width], 0, 0)
            early[pl.ds(first + (2 + h) * width, step), :] = part.astype(BF16)
        early[pl.ds(first + 4 * width, step), :] = dot(mixture[:, cols], branch[...], 0, 0).astype(BF16)


def reduce_kernel(
    orders, size,
    ray_normed, grad_queries, latent_normed, latent_all, grad_keys, grad_values, grad_hidden, rays,
    query_w, key_w, value_w, ray_gain, latent_gain, early, early_sums,
    ray_grad, latent_grad, summed, small,
    acc, landed, gathered, smalls, small_landed, latent_part, latent_landed, latent_mid,
    send_sem, recv_sem, back_send, back_recv, small_send, small_recv, latent_send, latent_recv, local_sem,
):
    bits = len(orders[0])
    partners = sorted(orders[0])
    width = rays.shape[1]
    early_rows = early.shape[0]
    greet(partners)
    load = pltpu.make_async_copy(early, acc.at[pl.ds(0, early_rows)], local_sem.at[0])
    load.start()

    def bit_of(partner):
        axis, bit = partner
        return lax.rem(lax.div(lax.axis_index(axis), bit), 2)

    groups = []
    for g, order in enumerate(orders):
        groups.append({"order": order, "start": g * size, "size": size, "base": g * size, "step": 0, "sends": [], "starts": [], "live": None})

    def remote(src, dst, send, recv, partner):
        return pltpu.make_async_remote_copy(
            src_ref=src, dst_ref=dst, send_sem=send, recv_sem=recv,
            device_id=peer(*partner), device_id_type=MESH,
        )

    def begin(g):
        group = groups[g]
        step = group["step"]
        partner = group["order"][step]
        half = group["size"] // 2
        mine = bit_of(partner)
        give = pl.multiple_of(group["start"] + (1 - mine) * half, 16)
        keep = pl.multiple_of(group["start"] + mine * half, 16)
        slot = group["base"] + size - group["size"]
        copy = remote(
            acc.at[pl.ds(give, half)], landed.at[pl.ds(slot, half)],
            send_sem.at[g * bits + step], recv_sem.at[g * bits + step], partner,
        )
        copy.start()
        group["live"] = (copy, keep, slot, half)
        group["starts"].append(group["start"])

    def finish(g):
        group = groups[g]
        copy, keep, slot, half = group["live"]
        copy.wait_recv()
        tile = min(half, 64)
        result = gathered if group["step"] == bits - 1 else acc

        @pl.loop(0, half // tile)
        def _(i):
            here = pl.ds(pl.multiple_of(keep + i * tile, 16), tile)
            there = pl.ds(pl.multiple_of(slot + i * tile, 16), tile)
            result[here, :] = (acc[here, :].astype(F32) + landed[there, :].astype(F32)).astype(BF16)

        copy.wait_send()
        group["start"], group["size"] = keep, half
        group["step"] += 1

    def begin_back(g):
        group = groups[g]
        step = group["step"] - 1
        partner = group["order"][step]
        rows = pl.ds(pl.multiple_of(group["start"], 16), group["size"])
        copy = remote(
            gathered.at[rows], gathered.at[rows],
            back_send.at[g * bits + step], back_recv.at[g * bits + step], partner,
        )
        copy.start()
        group["live"] = copy

    def finish_back(g):
        group = groups[g]
        group["live"].wait_recv()
        group["live"].wait_send()
        group["step"] -= 1
        group["start"] = group["starts"][group["step"]]
        group["size"] *= 2

    phase = [0] * len(groups)
    stores = []

    def advance(g):
        at = phase[g]
        phase[g] += 1
        if at == 0:
            begin(g)
        elif at < bits:
            finish(g)
            begin(g)
        elif at == bits:
            finish(g)
            begin_back(g)
        elif at < 2 * bits:
            finish_back(g)
            begin_back(g)
        elif at == 2 * bits:
            finish_back(g)
            rows = pl.ds(g * size, size)
            store = pltpu.make_async_copy(gathered.at[rows], summed.at[rows], local_sem.at[1 + g])
            store.start()
            stores.append(store)

    me = lax.axis_index("rays")
    lat = latent_landed.shape[1]
    near, far = ("rays", 1), ("rays", 2)

    smalls[0] = jnp.zeros(smalls.shape[1:], F32)
    smalls[0, 0:8, :] = early_sums[...]
    load.wait()
    ready = early_rows // size
    for g in range(ready):
        advance(g)

    for i in range(4):
        rows = slice(i * lat, (i + 1) * lat)
        part = dot(grad_keys[rows, :], key_w[...], 1, 1) + dot(grad_values[rows, :], value_w[...], 1, 1)
        standard, _ = stand(latent_all[rows, :].astype(F32))
        smalls[0, 8:9, :] += jnp.sum(part * standard, axis=0, keepdims=True)
        smalls[0, 9:10, :] += jnp.sum(part, axis=0, keepdims=True)
        latent_part[i] = part.astype(BF16)
    own_bit = lax.rem(me, 2)
    first_copies = []
    for i in range(2):
        copy = remote(
            latent_part.at[2 * i + 1 - own_bit], latent_landed.at[i], latent_send.at[i], latent_recv.at[i], near
        )
        copy.start()
        first_copies.append(copy)

    for g in range(ready):
        advance(g)

    step = 256
    for which, (left, right) in enumerate(
        ((ray_normed, grad_queries), (latent_normed, grad_keys), (latent_normed, grad_values))
    ):

        @pl.loop(0, width // step)
        def _(j):
            first = pl.multiple_of(j * step, step)
            part = dot(left[:, pl.ds(first, step)], right[...], 0, 0)
            acc[pl.ds(first + early_rows + which * width, step), :] = part.astype(BF16)

        if which == 0:
            for copy in first_copies:
                copy.wait_recv()
                copy.wait_send()
            other = lax.bitwise_xor(me, 2)
            sent = lax.div(other, 2)
            latent_mid[...] = (latent_part[other].astype(F32) + latent_landed[sent].astype(F32)).astype(BF16)
            second = remote(latent_mid, latent_landed.at[2], latent_send.at[2], latent_recv.at[2], far)
            second.start()
            for g in range(ready):
                advance(g)
    for g in range(ready, len(groups)):
        advance(g)

    chunk = 256

    @pl.loop(0, rays.shape[0] // chunk)
    def _(i):
        rows = pl.ds(pl.multiple_of(i * chunk, chunk), chunk)
        grad_normed = dot(grad_queries[rows, :], query_w[...], 1, 1)
        standard, inverse = stand(rays[rows, :].astype(F32))
        smalls[0, 6:7, :] += jnp.sum(grad_normed * standard, axis=0, keepdims=True)
        smalls[0, 7:8, :] += jnp.sum(grad_normed, axis=0, keepdims=True)
        ray_grad[rows, :] = (
            grad_hidden[rows, :] + norm_back(grad_normed, standard, inverse, ray_gain[...])
        ).astype(BF16)

    small_copies = []

    def small_begin(t):
        copy = remote(smalls.at[t], small_landed.at[t], small_send.at[t], small_recv.at[t], partners[t])
        copy.start()
        small_copies.append(copy)

    small_begin(0)
    for g in range(ready):
        advance(g)

    second.wait_recv()
    second.wait_send()
    own = lax.div(me, 2)
    grad_normed = (
        latent_part[me].astype(F32) + latent_landed[own].astype(F32) + latent_landed[2].astype(F32)
    )
    standard, inverse = stand(latent_all[pl.ds(pl.multiple_of(me * lat, 32), lat), :].astype(F32))
    latent_grad[...] = norm_back(grad_normed, standard, inverse, latent_gain[...]).astype(BF16)

    small_step = 0
    while any(at <= 2 * bits for at in phase):
        for g in range(len(groups)):
            advance(g)
        if small_step < bits:
            small_copies[small_step].wait_recv()
            smalls[small_step + 1] = smalls[small_step] + small_landed[small_step]
            small_copies[small_step].wait_send()
            small_step += 1
            if small_step < bits:
                small_begin(small_step)
    small[...] = smalls[bits]
    for store in stores:
        store.wait()


def log2(n):
    return n.bit_length() - 1


def ways(items, ray_parts):
    if (items, ray_parts) == (8, 4):
        core, y, x, z, zz = ("rays", 1), ("rays", 2), ("items", 1), ("items", 2), ("items", 4)
        a = (core, x, y, z, zz)
        b = (core, y, x, z, zz)
        c = (core, z, zz, x, y)
        return 1024, (a, b, c, a, b, c)
    order = tuple(("items", 1 << i) for i in range(log2(items))) + tuple(
        ("rays", 1 << i) for i in range(log2(ray_parts))
    )
    return 16 * items * ray_parts, (order,) * (6144 // (16 * items * ray_parts))


def on_device(
    items, ray_parts,
    rays, latents, ray_scene, latent_scene, latent_pad, cotangent,
    query_weight, key_weight, value_weight, out_weight, out_bias, up_weight, up_bias, down_weight, down_bias,
    ray_gain, ray_shift, latent_gain, latent_shift, mlp_gain, mlp_shift,
):
    _, count, width = rays.shape
    lat = latents.shape[1]
    total = lat * ray_parts
    padded = total + WINDOW
    hidden_width = up_weight.shape[1]
    x = rays[0]
    upstream = cotangent[0]

    def row(v):
        return v.reshape(1, -1)

    scene = ray_scene[0]
    order_key = scene * count + jnp.arange(count, dtype=jnp.int32)
    position = jnp.sum((order_key[None, :] < order_key[:, None]).astype(jnp.int32), axis=1)
    scene_list = jnp.arange(SCENES + 1, dtype=jnp.int32)
    ray_first = jnp.sum((scene[None, :] < scene_list[:, None]).astype(jnp.int32), axis=1)
    lat_first = jnp.sum(
        ((latent_scene[0][None, :] < scene_list[:, None]) & (latent_pad[0][None, :] == 0)).astype(jnp.int32), axis=1
    )
    block_first = jnp.arange(count // BLOCK, dtype=jnp.int32) * BLOCK

    def bound(at, edges):
        scene_at = jnp.sum((ray_first[None, 1:SCENES] <= at[:, None]).astype(jnp.int32), axis=1)
        return jnp.sum(jnp.where(scene_at[:, None] == scene_list[None, :SCENES], edges[None, :], 0), axis=1)

    low = bound(block_first, lat_first[:SCENES]) // 16 * 16
    high = bound(block_first + BLOCK - 1, lat_first[1:])
    windows = (high - low + WINDOW - 1) // WINDOW
    meta = jnp.concatenate([ray_first, lat_first, low, windows]).astype(jnp.int32)
    position_row = position.reshape(1, count)
    position_column = position.reshape(count, 1)

    big = functools.partial(pltpu.CompilerParams, vmem_limit_bytes=58 * MIB)
    shape = jax.ShapeDtypeStruct
    rows_bf16 = shape((count, width), BF16)

    ray_normed, queries, keys, values, latent_normed, latent_all = pl.pallas_call(
        project_kernel,
        out_shape=(
            rows_bf16, rows_bf16, shape((padded, width), BF16), shape((padded, width), BF16),
            shape((total, width), BF16), shape((total, width), BF16),
        ),
        in_specs=[vmem()] * 9,
        out_specs=[vmem()] * 6,
        scratch_shapes=[
            pltpu.VMEM((3, lat, width), BF16), pltpu.SemaphoreType.DMA((3,)), pltpu.SemaphoreType.DMA((3,)),
        ],
        compiler_params=big(collective_id=1, has_side_effects=True),
        name="project",
    )(
        x, latents[0], query_weight, key_weight, value_weight,
        row(ray_gain), row(ray_shift), row(latent_gain), row(latent_shift),
    )

    mixture, sorted_queries, sorted_mixture, log_total = pl.pallas_call(
        attend_kernel,
        out_shape=(rows_bf16, rows_bf16, rows_bf16, shape((count, 128), F32)),
        in_specs=[smem()] + [vmem()] * 5,
        out_specs=[vmem()] * 4,
        scratch_shapes=[
            pltpu.VMEM((padded, 128), BF16),
            pltpu.VMEM((PAIRS, 2 * BLOCK, 256), BF16),
            pltpu.VMEM((PAIRS, 2 * BLOCK, 256), F32),
            pltpu.VMEM((PAIRS, 2 * BLOCK, 1), F32),
        ],
        compiler_params=big(),
        name="attend",
    )(meta, queries, keys, values, position_row, position_column)

    ray_out, grad_mixture, grad_hidden, early, early_sums = pl.pallas_call(
        mlp_kernel,
        out_shape=(
            rows_bf16, rows_bf16, shape((count, width), F32),
            shape((2 * hidden_width + width, width), BF16), shape((8, width), F32),
        ),
        in_specs=[vmem()] * 11,
        out_specs=[vmem()] * 5,
        scratch_shapes=[
            pltpu.VMEM((count, hidden_width), BF16), pltpu.VMEM((count, hidden_width), BF16),
            pltpu.VMEM((count, width), BF16), pltpu.VMEM((count, width), BF16),
        ],
        compiler_params=big(),
        name="mlp",
    )(
        x, mixture, upstream, out_weight, up_weight, down_weight,
        row(out_bias), row(up_bias), row(down_bias), row(mlp_gain), row(mlp_shift),
    )

    grad_queries, grad_keys, grad_values = pl.pallas_call(
        attend_back_kernel,
        out_shape=(rows_bf16, shape((total, width), BF16), shape((total, width), BF16)),
        in_specs=[smem()] + [vmem()] * 8,
        out_specs=[vmem()] * 3,
        scratch_shapes=[
            pltpu.VMEM((padded, 128), BF16),
            pltpu.VMEM((PAIRS, 2 * BLOCK, 256), BF16),
            pltpu.VMEM((PAIRS, 2 * BLOCK, 256), BF16),
            pltpu.VMEM((count, width), BF16),
            pltpu.VMEM((padded, width), F32),
            pltpu.VMEM((padded, width), F32),
            pltpu.VMEM((PAIRS, 2 * BLOCK, 128), F32),
        ],
        compiler_params=big(),
        name="attend_back",
    )(
        meta, sorted_queries, keys, values, sorted_mixture, log_total, grad_mixture, position_row, position_column
    )

    size, orders = ways(items, ray_parts)
    bits, groups = len(orders[0]), len(orders)
    dma = pltpu.SemaphoreType.DMA
    rows_all = size * groups
    ray_grad, latent_grad, summed, small = pl.pallas_call(
        functools.partial(reduce_kernel, orders, size),
        out_shape=(
            rows_bf16, shape((lat, width), BF16), shape((rows_all, width), BF16), shape((16, width), F32),
        ),
        in_specs=[vmem()] * 13 + [anywhere(), vmem()],
        out_specs=[vmem(), vmem(), anywhere(), vmem()],
        scratch_shapes=[
            pltpu.VMEM((rows_all, width), BF16),
            pltpu.VMEM((rows_all, width), BF16),
            pltpu.VMEM((rows_all, width), BF16),
            pltpu.VMEM((bits + 1, 16, width), F32),
            pltpu.VMEM((bits, 16, width), F32),
            pltpu.VMEM((4, lat, width), BF16),
            pltpu.VMEM((3, lat, width), BF16),
            pltpu.VMEM((lat, width), BF16),
            dma((groups * bits,)), dma((groups * bits,)), dma((groups * bits,)), dma((groups * bits,)),
            dma((bits,)), dma((bits,)), dma((3,)), dma((3,)), dma((1 + groups,)),
        ],
        compiler_params=big(collective_id=2, has_side_effects=True),
        name="reduce",
    )(
        ray_normed, grad_queries, latent_normed, latent_all, grad_keys, grad_values, grad_hidden, x,
        query_weight, key_weight, value_weight, row(ray_gain), row(latent_gain), early, early_sums,
    )

    def part(i):
        return summed[i * width : (i + 1) * width].astype(F32)

    down_grad = summed[: 2 * width].astype(F32)
    up_grad = jnp.concatenate([part(2), part(3)], axis=1)
    return (
        ray_out[None], ray_grad[None], latent_grad[None],
        part(5), part(6), part(7), part(4), small[5],
        up_grad, small[1:3].reshape(-1), down_grad, small[0],
        small[6], small[7], small[8], small[9], small[3], small[4],
    )


def solution(mesh):
    split = P("items", "rays", None)
    in_specs = (split, split, P("items", "rays"), P("items", None), P("items", None), split) + (P(),) * 15
    out_specs = (split, split, split) + (P(),) * 15
    return jax.shard_map(
        functools.partial(on_device, mesh.shape["items"], mesh.shape["rays"]),
        mesh=mesh, in_specs=in_specs, out_specs=out_specs, check_vma=False,
    )
```

time: 898 us -> 350 us (0.39)
  waiting for transfers between devices: 343 us -> 0 us
  Pallas kernels: 0 us -> 313 us
  matrix products: 257 us -> 0 us
  other arithmetic: 121 us -> 19 us
  local copies, waits for them, and re-layouts: 111 us -> 17.8 us
  blocking collectives: 42.3 us -> 0 us
  between operations: 15.2 us -> 0.71 us
    pallas_call x0 -> x5, Pallas kernels: none -> 313 us  [the longest x1 145 us: on_device(): pl.pallas_call(functools.partial(reduce_kernel, orders, size), out_shape=...]
    dot_general x29 -> x0, matrix products: 257 us -> none  [the longest x4 67.2 us: masked_scores(): jnp.einsum('rhd,lhd->hrl', head_split(query_block), head_split(key_item),...]
    psum x1 -> x0, waiting for transfers between devices: 228 us -> none  [on_device(): lax.psum((query_grad, key_grad, value_grad, out_grad, out_bias_grad, up_g...]
    unnamed x4 -> x0, waiting for transfers between devices: 112 us -> none
    reduce_sum x12 -> x5, other arithmetic: 47.6 us -> 1.67 us  [the longest x1 0.81 us: on_device(): jnp.sum((scene[None, :] < scene_list[:, None]).astype(jnp.int32), axis=1)]
    convert_element_type x2 -> x1, other arithmetic: 46.8 us -> 4.21 us  [on_device(): down_grad = summed[:2 * width].astype(F32)]
    psum x1 -> x0, blocking collectives: 42.3 us -> none  [on_device(): lax.psum((query_grad, key_grad, value_grad, out_grad, out_bias_grad, up_g...]
    unnamed x144 -> x8, local copies, waits for them, and re-layouts: 35.6 us -> 2.07 us
  transfers between devices with their start and end apart: 3 -> 0, of which waited for: 3 -> 0; matrix products, arithmetic and copies ran while one was open for 9% -> 0% of each run, Pallas kernels for 0% -> 0%
where the time goes in v1:
time: 350 us
  Pallas kernels  313 us (89%)
  other arithmetic  19 us (5%)
  local copies, waits for them, and re-layouts  17.8 us (5%)
    pallas_call x1, Pallas kernels, on_device(): pl.pallas_call(functools.partial(reduce_kernel, orders, size), out_shape=...  145 us
    pallas_call x1, Pallas kernels, on_device(): pl.pallas_call(attend_kernel, out_shape=(rows_bf16, rows_bf16, rows_bf16,...  56.8 us
    pallas_call x1, Pallas kernels, on_device(): pl.pallas_call(attend_back_kernel, out_shape=(rows_bf16, shape((total, wi...  52.9 us
    pallas_call x1, Pallas kernels, on_device(): pl.pallas_call(mlp_kernel, out_shape=(rows_bf16, rows_bf16, shape((count,...  34.3 us
    pallas_call x1, Pallas kernels, on_device(): pl.pallas_call(project_kernel, out_shape=(rows_bf16, rows_bf16, shape((pa...  23.4 us
    reshape x9, local copies, waits for them, and re-layouts, row(): return v.reshape(1, -1)  11.4 us

profile of v1, /device:TPU:0, one launch (start us, length us, event | category | flops | bytes accessed | tf_op | source)
XLA Modules:
  0.0 350.0 jit_solution(3854632969794136094)
XLA Ops:
  0.7 0.8 convert_reduce_fusion.2
  1.5 0.1 slice.64
  1.5 0.1 convert_reduce_fusion.4
  1.6 0.7 compare_reduce_fusion
  2.4 1.3 reshape.97.ray_gain
  3.6 1.3 reshape.99.latent_gain
  4.9 1.3 reshape.103.out_bias
  6.2 1.3 reshape.105.down_bias
  7.4 1.3 reshape.98.ray_shift
  8.7 1.3 reshape.100.latent_shift
  10.0 1.3 reshape.106.mlp_gain
  11.2 1.3 reshape.107.mlp_shift
  12.5 0.7 iota_add_fusion
  13.2 0.7 iota_add_fusion.1
  13.9 0.6 convert_reduce_fusion
  14.4 0.0 copy-start.2
  14.4 1.3 reshape.104.up_bias
  15.7 0.7 reduce.1
  16.4 0.1 convert_reduce_fusion.1
  16.6 0.1 fusion.4
  16.7 0.1 select_reduce_fusion.1
  16.8 0.6 pad_add_fusion.meta
  17.4 1.0 copy.41.position_column
  18.4 23.4 %project.1 = (bf16[1024,768]{1,0:T(8,128)(2,1)}, bf16[1024,768]{1,0:T(8,128)(2,1)}, bf16[1408,768]{1,0:T(8,128)(2,1)}, bf16[1408,768]{1,0:T(8,128)(2,1)}, bf16[1...) custom-call(bf16[1024,768]{1,0:T(8,128)(2,1)} %bitcast.11, bf16[288,768]{1,0:T(8,128)(2,1)} %bitcast.16, ...), custom_call_target="tpu_custom_call" | custom-call | tf_op jit(solution)/shard_map/project/pallas_call | solution.py:654
  41.8 0.0 copy-done.2
  41.8 56.8 %attend.1 = (bf16[1024,768]{1,0:T(8,128)(2,1)}, bf16[1024,768]{1,0:T(8,128)(2,1)}, bf16[1024,768]{1,0:T(8,128)(2,1)}, f32[1024,128]{1,0:T(8,128)}) custom-call(s32[26]{0:T(128)} %pad_add_fusion.meta, bf16[1024,768]{1,0:T(8,128)(2,1)} %get-tuple-element.40.queries, bf16[1408,768]{1,0:T(8,128)(2,1)} %get-tuple-element.41.keys, ...), custom_call_target="tpu_custom_call" | custom-call | tf_op jit(solution)/shard_map/attend/pallas_call | solution.py:672
  98.6 34.3 %mlp.1 = (bf16[1024,768]{1,0:T(8,128)(2,1)}, bf16[1024,768]{1,0:T(8,128)(2,1)}, f32[1024,768]{1,0:T(8,128)}, bf16[3840,768]{1,0:T(8,128)(2,1)}, f32[8,768]{1,0:T(8,128)}) custom-call(bf16[1024,768]{1,0:T(8,128)(2,1)} %bitcast.12, bf16[1024,768]{1,0:T(8,128)(2,1)} %get-tuple-element.43.mixture, bf16[1024,768]{1,0:T(8,128)(2,1)} %bitcast.15, ...), custom_call_target="tpu_custom_call" | custom-call | tf_op jit(solution)/shard_map/mlp/pallas_call | solution.py:687
  133.0 52.9 %attend_back.1 = (bf16[1024,768]{1,0:T(8,128)(2,1)}, bf16[1152,768]{1,0:T(8,128)(2,1)}, bf16[1152,768]{1,0:T(8,128)(2,1)}) custom-call(s32[26]{0:T(128)} %pad_add_fusion.meta, bf16[1024,768]{1,0:T(8,128)(2,1)} %get-tuple-element.46.sorted_queries, bf16[1408,768]{1,0:T(8,128)(2,1)} %get-tuple-element.41.keys, bf16[1408,768]{1,0:T(8,128)(2,1)} %get-tuple-element.42.values, ...), custom_call_target="tpu_custom_call" | custom-call | tf_op jit(solution)/shard_map/attend_back/pallas_call | solution.py:706
  185.8 145.1 %reduce.20 = (bf16[1024,768]{1,0:T(8,128)(2,1)}, bf16[288,768]{1,0:T(8,128)(2,1)}, bf16[6144,768]{1,0:T(8,128)(2,1)}, f32[16,768]{1,0:T(8,128)}) custom-call(bf16[1024,768]{1,0:T(8,128)(2,1)} %get-tuple-element.45.ray_normed, bf16[1024,768]{1,0:T(8,128)(2,1)} %get-tuple-element.50.grad_queries, bf16[1152,768]{1,0:T(8,128)(2,1)} %get-tuple-element.51.latent_normed, ...), custom_call_target="tpu_custom_call" | custom-call | tf_op jit(solution)/shard_map/reduce/pallas_call | solution.py:730
  331.0 0.7 slice.75
  331.7 1.8 slice_reduce_fusion
  333.4 0.6 reshape.108
  334.1 4.2 %slice_convert_fusion = f32[1536,768]{1,0:T(8,128)} fusion(bf16[6144,768]{1,0:T(8,128)(2,1)} %get-tuple-element.60), kind=kLoop, calls=%fused_computation.2 | loop fusion | flops 1179648 | bytes 7077888 | tf_op jit(solution)/shard_map/convert_element_type | solution.py:759
  338.3 6.9 %fusion.3 = (bf16[768,768]{1,0:T(8,128)(2,1)S(1)}, bf16[768,768]{1,0:T(8,128)(2,1)S(1)}, f32[768,768]{1,0:T(8,128)}, f32[768,768]{1,0:T(8,128)}, f32[768,768]{1,0:T(8,128)}, /*index=5*/f32[768,768]{1,0:T(8,128)}) fusion(bf16[6144,768]{1,0:T(8,128)(2,1)} %get-tuple-element.60), kind=kLoop, calls=%fused_computation.39 | loop fusion | flops 2359296 | bytes 18874368 | tf_op jit(solution)/shard_map/slice | solution.py:757
  345.2 0.0 copy-start
  345.2 2.8 maximum_convert_fusion
  348.0 0.0 copy-done
  348.0 0.0 copy-start.1
  348.0 1.1 copy.45
  349.1 0.2 copy-done.1
  349.3 0.8 copy.46
  (3 shorter events, 0.0 us)
Async XLA Ops:
  14.4 27.4 %copy-start.2 = (s32[1024]{0:T(1024)}, s32[1024]{0:T(1024)S(1)}, u32[]{:S(2)}) copy-start(s32[1024]{0:T(1024)S(1)} %convert_reduce_fusion) | copy-start | bytes 12292
  345.2 2.8 copy-start
  348.0 1.3 copy-start.1

commit v2 on v1

v2 whole, which is shorter than its diff:
```python
import functools

import jax
import jax.numpy as jnp
from jax import lax
from jax.experimental import pallas as pl
from jax.experimental.pallas import tpu as pltpu
from jax.sharding import PartitionSpec as P

HEADS = 12
HEAD_DIM = 64
PAIRS = HEADS // 2
SCENES = 4
EPSILON = 1e-05
SCALE = HEAD_DIM ** (-0.5)
BLOCK = 128
WINDOW = 256
OUTSIDE = -1e30
MESH = pl.DeviceIdType.MESH
F32 = jnp.float32
BF16 = jnp.bfloat16
MIB = 2**20


def dot(left, right, left_dim=1, right_dim=0):
    return lax.dot_general(
        left, right, (((left_dim,), (right_dim,)), ((), ())), preferred_element_type=F32
    )


def stand(rows):
    center = rows - jnp.mean(rows, axis=-1, keepdims=True)
    inverse = lax.rsqrt(jnp.mean(center * center, axis=-1, keepdims=True) + EPSILON)
    return center * inverse, inverse


def norm_back(grad_out, standard, inverse, gain):
    scaled = grad_out * gain
    return inverse * (
        scaled
        - jnp.mean(scaled, axis=-1, keepdims=True)
        - standard * jnp.mean(scaled * standard, axis=-1, keepdims=True)
    )


def vmem():
    return pl.BlockSpec(memory_space=pltpu.VMEM)


def smem():
    return pl.BlockSpec(memory_space=pltpu.SMEM)


def anywhere():
    return pl.BlockSpec(memory_space=pl.ANY)


def peer(axis, bit):
    return {axis: lax.bitwise_xor(lax.axis_index(axis), bit)}


def greet(partners):
    barrier = pltpu.get_barrier_semaphore()
    for axis, bit in partners:
        pl.semaphore_signal(barrier, inc=1, device_id=peer(axis, bit), device_id_type=MESH)
    pl.semaphore_wait(barrier, len(partners))


def project_kernel(
    rays, latents, query_w, key_w, value_w, ray_gain, ray_shift, latent_gain, latent_shift,
    ray_normed, queries, keys, values, latent_normed, latent_all,
    landed, send_sem, recv_sem,
):
    me = lax.axis_index("rays")
    lat = latents.shape[0]
    near, far = ("rays", 1), ("rays", 2)
    greet([near, far])

    def copy(src, slot, partner, index):
        return pltpu.make_async_remote_copy(
            src_ref=src,
            dst_ref=landed.at[slot],
            send_sem=send_sem.at[index],
            recv_sem=recv_sem.at[index],
            device_id=peer(*partner),
            device_id_type=MESH,
        )

    to_far = copy(latents, 1, far, 1)
    to_near = copy(latents, 0, near, 0)
    to_far.start()
    to_near.start()

    chunk = 256

    @pl.loop(0, rays.shape[0] // chunk)
    def _(i):
        rows = pl.ds(pl.multiple_of(i * chunk, chunk), chunk)
        standard, _ = stand(rays[rows, :].astype(F32))
        normed = (standard * ray_gain[...] + ray_shift[...]).astype(BF16)
        ray_normed[rows, :] = normed
        projected = dot(normed, query_w[...]).astype(BF16)
        queries[rows, :] = (projected.astype(F32) * SCALE).astype(BF16)

    def one(raw, owner):
        rows = pl.ds(pl.multiple_of(owner * lat, 32), lat)
        latent_all[rows, :] = raw
        standard, _ = stand(raw.astype(F32))
        normed = (standard * latent_gain[...] + latent_shift[...]).astype(BF16)
        latent_normed[rows, :] = normed
        keys[rows, :] = dot(normed, key_w[...]).astype(BF16)
        values[rows, :] = dot(normed, value_w[...]).astype(BF16)

    total = 4 * lat
    keys[total:, :] = jnp.zeros((keys.shape[0] - total, keys.shape[1]), BF16)
    values[total:, :] = jnp.zeros((keys.shape[0] - total, keys.shape[1]), BF16)
    one(latents[...], me)
    to_far.wait_recv()
    passed = copy(landed.at[1], 2, near, 2)
    passed.start()
    to_near.wait_recv()
    one(landed[0], lax.bitwise_xor(me, 1))
    one(landed[1], lax.bitwise_xor(me, 2))
    passed.wait_recv()
    one(landed[2], lax.bitwise_xor(me, 3))
    to_far.wait_send()
    to_near.wait_send()
    passed.wait_send()


def lanes_of(shape):
    return lax.broadcasted_iota(jnp.int32, shape, len(shape) - 1)


def rows_of(shape):
    return lax.broadcasted_iota(jnp.int32, shape, 0)


def sort_plan(ray_scene, latent_scene, latent_pad, meta, position_row, position_column):
    count = ray_scene.shape[1]
    for s in range(1, SCENES):
        meta[s] = jnp.sum(jnp.where(ray_scene[...] < s, 1, 0))
    meta[0] = 0
    meta[SCENES] = count
    meta[SCENES + 1] = 0
    for s in range(1, SCENES + 1):
        meta[SCENES + 1 + s] = jnp.sum(jnp.where((latent_scene[...] < s) & (latent_pad[...] == 0), 1, 0))
    order_row = (ray_scene[...] * count + lanes_of((1, count))).astype(F32)
    order_column = jnp.broadcast_to(order_row, (8, count)).T[:, :1]
    step = 256
    smaller = jnp.zeros((1, count), F32)
    for i in range(count // step):
        before = jnp.where(order_column[i * step : (i + 1) * step] < order_row, 1.0, 0.0)
        smaller = smaller + jnp.sum(before, axis=0, keepdims=True)
    position_row[...] = smaller.astype(jnp.int32)
    position_column[...] = jnp.broadcast_to(smaller, (8, count)).T[:, :1].astype(jnp.int32)


def block_range(meta, block):
    first, last = block * BLOCK, block * BLOCK + BLOCK - 1
    low = sum(jnp.where(meta[s] <= first, 1, 0) for s in range(1, SCENES))
    high = sum(jnp.where(meta[s] <= last, 1, 0) for s in range(1, SCENES))
    start = meta[SCENES + 1 + low] // 16 * 16
    return start, (meta[SCENES + 2 + high] - start + WINDOW - 1) // WINDOW


def sort_rows(target, source, position_row):
    count = source.shape[0]
    step = 512

    @pl.loop(0, count // step)
    def _(i):
        first = pl.multiple_of(i * step, step)
        index = rows_of((step, count)) + first
        chosen = jnp.where(index == position_row[...], 1.0, 0.0).astype(BF16)
        target[pl.ds(first, step), :] = dot(chosen, source[...]).astype(BF16)


def unsort_rows(target, source, position_column):
    count = source.shape[0]
    step = 512

    @pl.loop(0, count // step)
    def _(i):
        first = pl.multiple_of(i * step, step)
        index = lanes_of((step, count))
        chosen = jnp.where(index == position_column[pl.ds(first, step), :], 1.0, 0.0).astype(BF16)
        target[pl.ds(first, step), :] = dot(chosen, source[...]).astype(BF16)


def latent_features(meta, extra, with_ones):
    shape = extra.shape
    row = rows_of(shape)
    lane = lanes_of((1, shape[1]))
    first = jnp.full((1, shape[1]), meta[SCENES + 1], jnp.int32)
    last = jnp.full((1, shape[1]), meta[SCENES + 2], jnp.int32)
    for s in range(1, SCENES):
        first = jnp.where(lane == s, meta[SCENES + 1 + s], first)
        last = jnp.where(lane == s, meta[SCENES + 2 + s], last)
    first = jnp.where(lane >= SCENES, 0, first)
    last = jnp.where(lane >= SCENES, shape[0], last)
    value = jnp.where((row >= first) & (row < last), 0.0, OUTSIDE)
    if with_ones:
        value = value + jnp.where((lane >= SCENES) & (lane < SCENES + 3), 1.0, 0.0)
    extra[...] = value.astype(BF16)


def ray_features(meta, block):
    shape = (BLOCK, 128)
    row = rows_of(shape) + block * BLOCK
    lane = lanes_of((1, 128))
    first = jnp.full((1, 128), count_none, jnp.int32)
    last = jnp.zeros((1, 128), jnp.int32)
    for s in range(SCENES):
        first = jnp.where(lane == s, meta[s], first)
        last = jnp.where(lane == s, meta[s + 1], last)
    return jnp.where((row >= first) & (row < last), 1.0, 0.0)


count_none = 2**30


def half_masks():
    lane = lanes_of((BLOCK, 128))
    low = jnp.where(lane < HEAD_DIM, 1.0, 0.0)
    return low, 1.0 - low


def pick_halves(both):
    lane = lanes_of((BLOCK, 128))
    return jnp.where(lane < HEAD_DIM, both[:BLOCK, :128], both[BLOCK:, :128])


def pair_columns(p):
    return slice(128 * p, 128 * (p + 1))


def attend_kernel(
    queries, keys, values, ray_scene, latent_scene, latent_pad,
    mixture, sorted_queries, sorted_mixture, log_total, meta, position_row, position_column,
    latent_extra, stacked, total, peak, held,
):
    rays = queries.shape[0]
    sort_plan(ray_scene, latent_scene, latent_pad, meta, position_row, position_column)
    latent_features(meta, latent_extra, False)
    sort_rows(sorted_queries, queries, position_row)
    ones = jnp.where(lanes_of((WINDOW, 128)) == 0, 1.0, 0.0).astype(BF16)
    low, high = half_masks()
    lane = lanes_of((BLOCK, 128))

    @pl.loop(0, rays // BLOCK)
    def _(block):
        rows = pl.ds(pl.multiple_of(block * BLOCK, BLOCK), BLOCK)
        start, windows = block_range(meta, block)
        extra = ray_features(meta, block).astype(BF16)
        for p in range(PAIRS):
            pair = sorted_queries[rows, pair_columns(p)].astype(F32)
            stacked[p, :BLOCK, :128] = (pair * low).astype(BF16)
            stacked[p, BLOCK:, :128] = (pair * high).astype(BF16)
            stacked[p, :BLOCK, 128:] = extra
            stacked[p, BLOCK:, 128:] = extra
            peak[p] = jnp.full((2 * BLOCK, 128), -3e38, F32)
            total[p] = jnp.zeros((2 * BLOCK, 256), F32)

        @pl.loop(0, windows)
        def _(w):
            window = pl.ds(pl.multiple_of(start + w * WINDOW, 16), WINDOW)
            extra_keys = latent_extra[window, :]
            for p in range(PAIRS):
                key_side = jnp.concatenate([keys[window, pair_columns(p)], extra_keys], axis=1)
                scores = dot(stacked[p], key_side, 1, 1)
                held[w, p] = scores
                peak[p] = jnp.maximum(peak[p], jnp.maximum(scores[:, :128], scores[:, 128:]))

        for p in range(PAIRS):
            peak[p] = jnp.broadcast_to(jnp.max(peak[p], axis=1, keepdims=True), (2 * BLOCK, 128))

        @pl.loop(0, windows)
        def _(w):
            window = pl.ds(pl.multiple_of(start + w * WINDOW, 16), WINDOW)
            for p in range(PAIRS):
                top = peak[p]
                lifted = jnp.exp(held[w, p] - jnp.concatenate([top, top], axis=1)).astype(BF16)
                value_side = jnp.concatenate([values[window, pair_columns(p)], ones], axis=1)
                total[p] += dot(lifted, value_side)

        logs = jnp.zeros((BLOCK, 128), F32)
        for p in range(PAIRS):
            both = total[p]
            sums = both[:, 128:129]
            mixed = pick_halves(both[:, :128] * (1.0 / sums))
            sorted_mixture[rows, pair_columns(p)] = mixed.astype(BF16)
            log_rows = peak[p] + jnp.log(sums)
            logs = jnp.where(lane == 2 * p, log_rows[:BLOCK], logs)
            logs = jnp.where(lane == 2 * p + 1, log_rows[BLOCK:], logs)
        log_total[rows, :] = logs

    unsort_rows(mixture, sorted_mixture, position_column)


def three_parts(column, first_lane):
    lane = lanes_of((BLOCK, 128))
    value = -column
    top = value.astype(BF16).astype(F32)
    rest = value - top
    middle = rest.astype(BF16).astype(F32)
    lowest = rest - middle
    out = jnp.where(lane == first_lane, top, 0.0)
    out = jnp.where(lane == first_lane + 1, middle, out)
    return jnp.where(lane == first_lane + 2, lowest, out)


def attend_back_kernel(
    meta, sorted_queries, keys, values, sorted_mixture, log_total, grad_mixture, position_row, position_column,
    grad_queries, grad_keys, grad_values,
    latent_extra, stacked, stacked_grad, sorted_grad, key_total, value_total, query_total, probs_low, scores_low,
):
    rays = sorted_queries.shape[0]
    latent_features(meta, latent_extra, True)
    sort_rows(sorted_grad, grad_mixture, position_row)
    ones = jnp.where(lanes_of((WINDOW, 128)) < 3, 1.0, 0.0).astype(BF16)
    low, high = half_masks()
    key_total[...] = jnp.zeros(key_total.shape, F32)
    value_total[...] = jnp.zeros(value_total.shape, F32)

    @pl.loop(0, rays // BLOCK)
    def _(block):
        rows = pl.ds(pl.multiple_of(block * BLOCK, BLOCK), BLOCK)
        start, windows = block_range(meta, block)
        extra = ray_features(meta, block)
        logs = log_total[rows, :]
        for p in range(PAIRS):
            columns = pair_columns(p)
            pair = sorted_queries[rows, columns].astype(F32)
            grad = sorted_grad[rows, columns].astype(F32)
            product = grad * sorted_mixture[rows, columns].astype(F32)
            for side, mask in enumerate((low, high)):
                half = slice(side * BLOCK, (side + 1) * BLOCK)
                head = 2 * p + side
                stacked[p, half, :128] = (pair * mask).astype(BF16)
                stacked[p, half, 128:] = (extra + three_parts(logs[:, head : head + 1], SCENES)).astype(BF16)
                inner = jnp.sum(product * mask, axis=1, keepdims=True)
                stacked_grad[p, half, :128] = (grad * mask).astype(BF16)
                stacked_grad[p, half, 128:] = three_parts(inner, 0).astype(BF16)
            query_total[p] = jnp.zeros((2 * BLOCK, 128), F32)

        @pl.loop(0, windows)
        def _(w):
            window = pl.ds(pl.multiple_of(start + w * WINDOW, 16), WINDOW)
            extra_keys = latent_extra[window, :]
            for p in range(PAIRS):
                columns = pair_columns(p)
                probs = jnp.exp(dot(jnp.concatenate([keys[window, columns], extra_keys], axis=1), stacked[p], 1, 1))
                value_side = jnp.concatenate([values[window, columns], ones], axis=1)
                centered = dot(value_side, stacked_grad[p], 1, 1)
                probs_low[p] = probs.astype(BF16)
                scores_low[p] = (probs * centered).astype(BF16)
            for p in range(PAIRS):
                columns = pair_columns(p)
                value_total[window, columns] += dot(probs_low[p], stacked_grad[p, :, :128])
                key_total[window, columns] += dot(scores_low[p], stacked[p, :, :128])
                query_total[p] += dot(scores_low[p], keys[window, columns], 0, 0)

        for p in range(PAIRS):
            sorted_grad[rows, pair_columns(p)] = (pick_halves(query_total[p]) * SCALE).astype(BF16)

    unsort_rows(grad_queries, sorted_grad, position_column)
    count = grad_keys.shape[0]
    grad_keys[...] = key_total[:count, :].astype(BF16)
    grad_values[...] = value_total[:count, :].astype(BF16)


def big(**rest):
    return pltpu.CompilerParams(vmem_limit_bytes=60 * MIB, **rest)


def run_attend(queries, keys, values, ray_scene, latent_scene, latent_pad):
    count, width = queries.shape
    padded = keys.shape[0]
    shape = jax.ShapeDtypeStruct
    rows_bf16 = shape((count, width), BF16)
    most = (padded - 1) // WINDOW + 1
    return pl.pallas_call(
        attend_kernel,
        out_shape=(
            rows_bf16, rows_bf16, rows_bf16, shape((count, 128), F32), shape((2 * SCENES + 2,), jnp.int32),
            shape((1, count), jnp.int32), shape((count, 1), jnp.int32),
        ),
        in_specs=[vmem()] * 6,
        out_specs=[vmem()] * 4 + [smem(), vmem(), vmem()],
        scratch_shapes=[
            pltpu.VMEM((padded, 128), BF16),
            pltpu.VMEM((PAIRS, 2 * BLOCK, 256), BF16),
            pltpu.VMEM((PAIRS, 2 * BLOCK, 256), F32),
            pltpu.VMEM((PAIRS, 2 * BLOCK, 128), F32),
            pltpu.VMEM((most, PAIRS, 2 * BLOCK, WINDOW), F32),
        ],
        compiler_params=big(),
        name="attend",
    )(queries, keys, values, ray_scene, latent_scene, latent_pad)


def mix_of(forward):
    return forward[0]


def run_attend_back(forward, keys, values, grad_mixture, *_):
    _, sorted_queries, sorted_mixture, log_total, meta, position_row, position_column = forward
    count, width = grad_mixture.shape
    padded = keys.shape[0]
    total = padded - WINDOW
    shape = jax.ShapeDtypeStruct
    return pl.pallas_call(
        attend_back_kernel,
        out_shape=(shape((count, width), BF16), shape((total, width), BF16), shape((total, width), BF16)),
        in_specs=[smem()] + [vmem()] * 8,
        out_specs=[vmem()] * 3,
        scratch_shapes=[
            pltpu.VMEM((padded, 128), BF16),
            pltpu.VMEM((PAIRS, 2 * BLOCK, 256), BF16),
            pltpu.VMEM((PAIRS, 2 * BLOCK, 256), BF16),
            pltpu.VMEM((count, width), BF16),
            pltpu.VMEM((padded, width), F32),
            pltpu.VMEM((padded, width), F32),
            pltpu.VMEM((PAIRS, 2 * BLOCK, 128), F32),
            pltpu.VMEM((PAIRS, WINDOW, 2 * BLOCK), BF16),
            pltpu.VMEM((PAIRS, WINDOW, 2 * BLOCK), BF16),
        ],
        compiler_params=big(),
        name="attend_back",
    )(meta, sorted_queries, keys, values, sorted_mixture, log_total, grad_mixture, position_row, position_column)


def bit_of(partner):
    axis, bit = partner
    return lax.rem(lax.div(lax.axis_index(axis), bit), 2)


def remote(src, dst, send, recv, partner):
    return pltpu.make_async_remote_copy(
        src_ref=src, dst_ref=dst, send_sem=send, recv_sem=recv, device_id=peer(*partner), device_id_type=MESH
    )


def part_start(order, size, flipped=()):
    start = 0
    for i, partner in enumerate(order[:2]):
        mine = bit_of(partner)
        if partner in flipped:
            mine = 1 - mine
        start = start + mine * (size >> (i + 1))
    return start


def mlp_kernel(
    core, orders, size,
    rays, mixture, cotangent, out_w, up_w, down_w, out_bias, up_bias, down_bias, mlp_gain, mlp_shift,
    ray_out, grad_mixture, grad_hidden, quarters, sums,
    act, grad_pre, normed, branch, early, landed, send_sem, recv_sem,
):
    chunk = 256
    width = rays.shape[1]
    half_width = width // 2
    greet([core])
    mine = bit_of(core)
    sums[...] = jnp.zeros(sums.shape, F32)
    root = 0.7978845608028654
    cubic = 0.044715

    @pl.loop(0, rays.shape[0] // chunk)
    def _(i):
        rows = pl.ds(pl.multiple_of(i * chunk, chunk), chunk)
        hidden = rays[rows, :].astype(F32) + dot(mixture[rows, :], out_w[...]) + out_bias[...]
        standard, inverse = stand(hidden)
        low = (standard * mlp_gain[...] + mlp_shift[...]).astype(BF16)
        normed[rows, :] = low
        upstream = cotangent[rows, :]
        half = 768
        out = hidden + down_bias[...]
        grad_mlp = jnp.zeros((chunk, width), F32)
        for j in range(up_w.shape[1] // half):
            cols = slice(j * half, (j + 1) * half)
            pre = dot(low, up_w[:, cols]) + up_bias[:, cols]
            square = pre * pre
            bend = jnp.tanh(root * pre * (1.0 + cubic * square))
            rise = 0.5 * (1.0 + bend)
            active = (pre * rise).astype(BF16)
            slope = rise + 0.5 * pre * (1.0 - bend * bend) * (root * (1.0 + 3.0 * cubic * square))
            act[rows, cols] = active
            out = out + dot(active, down_w[cols, :])
            back = (dot(upstream, down_w[cols, :], 1, 1) * slope).astype(BF16)
            grad_pre[rows, cols] = back
            sums[1 + j : 2 + j, :] += jnp.sum(back.astype(F32), axis=0, keepdims=True)
            grad_mlp = grad_mlp + dot(back, up_w[:, cols], 1, 1)
        ray_out[rows, :] = out.astype(BF16)
        wide = upstream.astype(F32)
        sums[0:1, :] += jnp.sum(wide, axis=0, keepdims=True)
        sums[3:4, :] += jnp.sum(grad_mlp * standard, axis=0, keepdims=True)
        sums[4:5, :] += jnp.sum(grad_mlp, axis=0, keepdims=True)
        through = wide + norm_back(grad_mlp, standard, inverse, mlp_gain[...])
        grad_hidden[rows, :] = through
        rounded = through.astype(BF16)
        branch[rows, :] = rounded
        sums[5:6, :] += jnp.sum(rounded.astype(F32), axis=0, keepdims=True)
        grad_mixture[rows, :] = dot(rounded, out_w[...], 1, 1).astype(BF16)

    step = 256
    tiles = width // step

    def swap(tile):
        rows = pl.ds(pl.multiple_of(lax.div(tile, tiles) * size + lax.rem(tile, tiles) * step, step), step)
        return remote(early.at[1 - mine, rows], landed.at[rows], send_sem.at[tile], recv_sem.at[tile], core)

    def store(tile, left, right):
        rows = pl.ds(pl.multiple_of(lax.div(tile, tiles) * size + lax.rem(tile, tiles) * step, step), step)
        part = dot(left, right, 0, 0).astype(BF16)
        early[0, rows, :] = part[:, :half_width]
        early[1, rows, :] = part[:, half_width:]
        swap(tile).start()

    @pl.loop(0, 2 * tiles)
    def _(j):
        store(j, act[:, pl.ds(pl.multiple_of(j * step, step), step)], cotangent[...])

    for h in range(2):

        @pl.loop(0, tiles)
        def _(j):
            cols = pl.ds(pl.multiple_of(j * step, step), step)
            store(j + (2 + h) * tiles, normed[:, cols], grad_pre[:, h * width : (h + 1) * width])

    @pl.loop(0, tiles)
    def _(j):
        store(j + 4 * tiles, mixture[:, pl.ds(pl.multiple_of(j * step, step), step)], branch[...])

    @pl.loop(0, 5 * tiles)
    def _(tile):
        swap(tile).wait_recv()

    quarter = size // 4
    for g, order in enumerate(orders):
        first, second = sorted(order[:2])
        for target, flipped in enumerate(((), (first,), (second,), (first, second))):
            start = pl.multiple_of(g * size + part_start(order, size, flipped), 16)
            rows = pl.ds(start, quarter)
            quarters[target, g] = (early[mine, rows, :].astype(F32) + landed[rows, :].astype(F32)).astype(BF16)

    @pl.loop(0, 5 * tiles)
    def _(tile):
        swap(tile).wait_send()


def reduce_kernel(
    core, orders, size, script, early_groups,
    quarters, from_first, from_second, from_both,
    latent_normed, grad_keys, grad_values, key_w, value_w, latent_all,
    ray_normed, grad_queries, query_w, rays, grad_hidden,
    ray_gain, latent_gain, early_sums,
    ray_grad, latent_grad, summed, small,
    v_quarters, v_first, v_second, v_both,
    v_latent_normed, v_grad_keys, v_grad_values, v_key_w, v_value_w, v_latent_all,
    v_ray_normed, v_grad_queries, v_query_w, v_rays, v_grad_hidden,
    late, late_landed, acc, landed, gathered,
    smalls, small_landed, latent_part, latent_landed, latent_mid,
    load_sem, swap_send, swap_recv, send_sem, recv_sem, back_send, back_recv,
    small_send, small_recv, latent_send, latent_recv, store_sem,
):
    bits = len(orders[0])
    partners = sorted(orders[0] + (core,))
    width = rays.shape[1]
    half_width = width // 2
    quarter = size // 4
    held = (
        v_quarters, v_first, v_second, v_both,
        v_latent_normed, v_grad_keys, v_grad_values, v_key_w, v_value_w, v_latent_all,
        v_ray_normed, v_grad_queries, v_query_w, v_rays, v_grad_hidden,
    )
    given = (
        quarters.at[0], from_first, from_second, from_both,
        latent_normed, grad_keys, grad_values, key_w, value_w, latent_all,
        ray_normed, grad_queries, query_w, rays, grad_hidden,
    )
    loads = [pltpu.make_async_copy(src, dst, load_sem.at[i]) for i, (src, dst) in enumerate(zip(given, held))]
    for load in loads:
        load.start()
    greet(partners)
    mine = bit_of(core)
    loaded = [0]

    def need(count):
        while loaded[0] < count:
            loads[loaded[0]].wait()
            loaded[0] += 1

    smalls[0] = jnp.zeros(smalls.shape[1:], F32)
    smalls[0, 0:8, :] = early_sums[...]


    class Group:
        pass

    groups = []
    for g, order in enumerate(orders):
        group = Group()
        group.order, group.start, group.size, group.step, group.starts, group.live = order, g * size, size, 0, [], None
        group.index, group.at, group.shift = g, 0, early_groups * (size - quarter)
        groups.append(group)

    def rows_at(start, count):
        return pl.ds(pl.multiple_of(start, 16), count)

    def add_rows(target, there, first, second, here, count):
        tile = next(t for t in (64, 48, 32, 16) if count % t == 0)

        @pl.loop(0, count // tile)
        def _(i):
            one = first[rows_at(here[0] + i * tile, tile), :].astype(F32)
            two = second[rows_at(here[1] + i * tile, tile), :].astype(F32)
            target[rows_at(there + i * tile, tile), :] = (one + two).astype(BF16)

    def swap_begin(group):
        rows = rows_at((group.index - early_groups) * size, size)
        i = group.index - early_groups
        group.live = remote(late.at[1 - mine, rows], late_landed.at[rows], swap_send.at[i], swap_recv.at[i], core)
        group.live.start()

    def swap_finish(group):
        group.live.wait_recv()
        base = (group.index - early_groups) * size
        add_rows(acc, group.start - group.shift, late.at[mine], late_landed, (base, base), size)
        group.live.wait_send()

    def halve_begin(group):
        partner = group.order[group.step]
        half = group.size // 2
        bit = bit_of(partner)
        give, keep = group.start + (1 - bit) * half, group.start + bit * half
        if group.index < early_groups:
            slot = (group.index + 1) * quarter - group.size
        else:
            slot = early_groups * quarter + (group.index - early_groups + 1) * size - group.size
        i = group.index * bits + group.step
        copy = remote(
            acc.at[rows_at(give - group.shift, half)], landed.at[rows_at(slot, half)], send_sem.at[i], recv_sem.at[i], partner
        )
        copy.start()
        group.starts.append(group.start)
        group.live = (copy, keep, slot, half)

    def halve_finish(group):
        copy, keep, slot, half = group.live
        copy.wait_recv()
        last = group.step == bits - 1
        here = keep - group.shift
        add_rows(gathered.at[mine] if last else acc, keep if last else here, acc, landed, (here, slot), half)
        copy.wait_send()
        group.start, group.size = keep, half
        group.step += 1

    def double_begin(group):
        rows = rows_at(group.start, group.size)
        step = group.step - 1
        i = group.index * (bits + 1) + step + 1
        partner = group.order[step] if step >= 0 else core
        piece = gathered.at[mine, rows]
        group.live = remote(piece, piece, back_send.at[i], back_recv.at[i], partner)
        group.live.start()

    def double_finish(group):
        group.live.wait_recv()
        group.live.wait_send()
        group.step -= 1
        if group.step >= 0:
            group.start = group.starts[group.step]
            group.size *= 2

    stores = []

    def store(group):
        rows = pl.ds(group.index * size, size)
        for side in range(2):
            copy = pltpu.make_async_copy(
                gathered.at[side, rows], summed.at[side, rows], store_sem.at[2 * group.index + side]
            )
            copy.start()
            stores.append(copy)

    def plan(group):
        steps = []
        halvings = bits
        if group.index < early_groups:
            halvings = bits - 2
        else:
            steps.append((swap_begin, swap_finish))
        steps += [(halve_begin, halve_finish)] * halvings
        steps += [(double_begin, double_finish)] * (bits + 1)
        return steps

    plans = [plan(group) for group in groups]

    def advance(g):
        group, steps = groups[g], plans[g]
        if group.at > 0:
            steps[group.at - 1][1](group)
        if group.at < len(steps):
            steps[group.at][0](group)
        else:
            store(group)
        group.at += 1


    me = lax.axis_index("rays")
    lat = latent_mid.shape[0]
    near, far = ("rays", 1), ("rays", 2)
    near_copies = [
        remote(latent_part.at[2 * i + 1 - lax.rem(me, 2)], latent_landed.at[i], latent_send.at[i], latent_recv.at[i], near)
        for i in range(2)
    ]
    far_copy = remote(latent_mid, latent_landed.at[2], latent_send.at[2], latent_recv.at[2], far)
    small_copies = [
        remote(smalls.at[t], small_landed.at[t], small_send.at[t], small_recv.at[t], partners[t])
        for t in range(bits + 1)
    ]

    def early_begin():
        need(4)
        for g in range(early_groups):
            group = groups[g]
            start = g * size
            for i, partner in enumerate(group.order[:2]):
                group.starts.append(start)
                start = start + bit_of(partner) * (size >> (i + 1))
            group.start, group.size, group.step, group.shift = start, quarter, 2, start - g * quarter
            total = v_quarters[g].astype(F32) + v_first[g].astype(F32) + v_second[g].astype(F32) + v_both[g].astype(F32)
            acc[pl.ds(g * quarter, quarter), :] = total.astype(BF16)
            advance(g)

    step = 256

    def weight_grad(index, left, right):
        @pl.loop(0, width // step)
        def _(j):
            first = pl.multiple_of(j * step, step)
            part = dot(left[:, pl.ds(first, step)], right[...], 0, 0).astype(BF16)
            rows = pl.ds(pl.multiple_of(index * size + first, step), step)
            late[0, rows, :] = part[:, :half_width]
            late[1, rows, :] = part[:, half_width:]

        advance(early_groups + index)

    def query_part():
        need(12)
        weight_grad(0, v_ray_normed, v_grad_queries)

    def key_part():
        need(6)
        weight_grad(1, v_latent_normed, v_grad_keys)

    def value_part():
        need(7)
        weight_grad(2, v_latent_normed, v_grad_values)

    def latents_begin():
        need(10)
        for i in range(4):
            rows = slice(i * lat, (i + 1) * lat)
            part = dot(v_grad_keys[rows, :], v_key_w[...], 1, 1) + dot(v_grad_values[rows, :], v_value_w[...], 1, 1)
            standard, _ = stand(v_latent_all[rows, :].astype(F32))
            smalls[0, 8:9, :] += jnp.sum(part * standard, axis=0, keepdims=True)
            smalls[0, 9:10, :] += jnp.sum(part, axis=0, keepdims=True)
            latent_part[i] = part.astype(BF16)
        for copy in near_copies:
            copy.start()

    def latents_next():
        for copy in near_copies:
            copy.wait_recv()
            copy.wait_send()
        other = lax.bitwise_xor(me, 2)
        latent_mid[...] = (
            latent_part[other].astype(F32) + latent_landed[lax.div(other, 2)].astype(F32)
        ).astype(BF16)
        far_copy.start()

    def latents_end():
        far_copy.wait_recv()
        far_copy.wait_send()
        grad_normed = (
            latent_part[me].astype(F32) + latent_landed[lax.div(me, 2)].astype(F32) + latent_landed[2].astype(F32)
        )
        standard, inverse = stand(v_latent_all[pl.ds(pl.multiple_of(me * lat, 32), lat), :].astype(F32))
        latent_grad[...] = norm_back(grad_normed, standard, inverse, latent_gain[...]).astype(BF16)

    def rays_part():
        need(15)
        chunk = 256

        @pl.loop(0, rays.shape[0] // chunk)
        def _(i):
            rows = pl.ds(pl.multiple_of(i * chunk, chunk), chunk)
            grad_normed = dot(v_grad_queries[rows, :], v_query_w[...], 1, 1)
            standard, inverse = stand(v_rays[rows, :].astype(F32))
            smalls[0, 6:7, :] += jnp.sum(grad_normed * standard, axis=0, keepdims=True)
            smalls[0, 7:8, :] += jnp.sum(grad_normed, axis=0, keepdims=True)
            ray_grad[rows, :] = (
                v_grad_hidden[rows, :] + norm_back(grad_normed, standard, inverse, ray_gain[...])
            ).astype(BF16)

        small_copies[0].start()

    small_at = [0]

    def small_next():
        t = small_at[0]
        small_copies[t].wait_recv()
        smalls[t + 1] = smalls[t] + small_landed[t]
        small_copies[t].wait_send()
        small_at[0] += 1
        if t + 1 <= bits:
            small_copies[t + 1].start()
        else:
            small[...] = smalls[bits + 1]

    tasks = {
        "E": early_begin, "Q": query_part, "K": key_part, "V": value_part, "L": latents_begin, "M": latents_next,
        "N": latents_end, "R": rays_part, "S": small_next,
    }
    for letter in script:
        if letter in tasks:
            tasks[letter]()
        else:
            advance(int(letter))
    while small_at[0] <= bits:
        small_next()
    while any(group.at <= len(steps) for group, steps in zip(groups, plans)):
        for g in range(len(groups)):
            if groups[g].at <= len(plans[g]):
                advance(g)
    for copy in stores:
        copy.wait()


def widen_kernel(size, summed, *refs):
    down, up, out, query, key, value, held, wide, load_sem, store_sem = refs
    width = held.shape[3] * 2
    half = width // 2
    step = held.shape[2]
    jobs = []
    for g in range(8):
        for r in range(0, width, step):
            if g < 2:
                target = down.at[pl.ds(g * width + r, step), :]
            elif g < 4:
                target = up.at[pl.ds(r, step), pl.ds((g - 2) * width, width)]
            else:
                target = (out, query, key, value)[g - 4].at[pl.ds(r, step), :]
            jobs.append((summed.at[:, pl.ds(g * size + r, step), :], target))
    slots = held.shape[0]
    loads = [pltpu.make_async_copy(src, held.at[i % slots], load_sem.at[i % slots]) for i, (src, _) in enumerate(jobs)]
    saves = [pltpu.make_async_copy(wide.at[i % slots], dst, store_sem.at[i % slots]) for i, (_, dst) in enumerate(jobs)]
    for i in range(slots):
        loads[i].start()
    for i in range(len(jobs)):
        slot = i % slots
        loads[i].wait()
        if i >= slots:
            saves[i - slots].wait()
        wide[slot, :, :half] = held[slot, 0].astype(F32)
        wide[slot, :, half:] = held[slot, 1].astype(F32)
        saves[i].start()
        if i + slots < len(jobs):
            loads[i + slots].start()
    for i in range(len(jobs) - slots, len(jobs)):
        saves[i].wait()


def log2(n):
    return n.bit_length() - 1


EARLY = 5


def ways(items, ray_parts):
    core, y, x = ("rays", 1), ("rays", 2), ("items", 1)
    others = tuple(("items", 2 << i) for i in range(log2(items) - 1)) + tuple(
        ("rays", 4 << i) for i in range(log2(ray_parts) - 2)
    )
    a, b, c, d = (x, y) + others, (y, x) + others, (x, y) + others[::-1], (y, x) + others[::-1]
    orders = (a, d, b, c, a, d, a, c)
    return core, x, y, orders, "EKVQL0126M73451RN0S27615S4036S1275S04S"


def on_device(
    items, ray_parts,
    rays, latents, ray_scene, latent_scene, latent_pad, cotangent,
    query_weight, key_weight, value_weight, out_weight, out_bias, up_weight, up_bias, down_weight, down_bias,
    ray_gain, ray_shift, latent_gain, latent_shift, mlp_gain, mlp_shift,
):
    _, count, width = rays.shape
    lat = latents.shape[1]
    total = lat * ray_parts
    padded = total + WINDOW
    hidden_width = up_weight.shape[1]
    x = rays[0]
    upstream = cotangent[0]

    def row(v):
        return v.reshape(1, -1)

    shape = jax.ShapeDtypeStruct
    rows_bf16 = shape((count, width), BF16)
    total_bf16 = shape((total, width), BF16)
    dma = pltpu.SemaphoreType.DMA

    ray_normed, queries, keys, values, latent_normed, latent_all = pl.pallas_call(
        project_kernel,
        out_shape=(
            rows_bf16, rows_bf16, shape((padded, width), BF16), shape((padded, width), BF16), total_bf16, total_bf16,
        ),
        in_specs=[vmem()] * 9,
        out_specs=[vmem()] * 6,
        scratch_shapes=[pltpu.VMEM((3, lat, width), BF16), dma((3,)), dma((3,))],
        compiler_params=big(collective_id=1, has_side_effects=True),
        name="project",
    )(
        x, latents[0], query_weight, key_weight, value_weight,
        row(ray_gain), row(ray_shift), row(latent_gain), row(latent_shift),
    )

    forward = run_attend(queries, keys, values, ray_scene, latent_scene, latent_pad)
    mixture = forward[0]

    core, first, second, orders, script = ways(items, ray_parts)
    bits = len(orders[0])
    unit = 16 << bits
    size = (width + unit - 1) // unit * unit
    quarter = size // 4
    half_width = width // 2
    groups = len(orders)
    late_groups = groups - EARLY
    quarter_bf16 = (EARLY, quarter, half_width)

    ray_out, grad_mixture, grad_hidden, quarters, early_sums = pl.pallas_call(
        functools.partial(mlp_kernel, core, orders[:EARLY], size),
        out_shape=(
            rows_bf16, rows_bf16, shape((count, width), F32), shape((4,) + quarter_bf16, BF16), shape((8, width), F32),
        ),
        in_specs=[vmem()] * 11,
        out_specs=[vmem()] * 5,
        scratch_shapes=[
            pltpu.VMEM((count, hidden_width), BF16), pltpu.VMEM((count, hidden_width), BF16),
            pltpu.VMEM((count, width), BF16), pltpu.VMEM((count, width), BF16),
            pltpu.VMEM((2, EARLY * size, half_width), BF16), pltpu.VMEM((EARLY * size, half_width), BF16),
            dma((15,)), dma((15,)),
        ],
        compiler_params=big(collective_id=2, has_side_effects=True),
        name="mlp",
    )(
        x, mixture, upstream, out_weight, up_weight, down_weight,
        row(out_bias), row(up_bias), row(down_bias), row(mlp_gain), row(mlp_shift),
    )

    def flip(index, partners):
        item, part = index // ray_parts, index % ray_parts
        for axis, bit in partners:
            item, part = (item ^ bit, part) if axis == "items" else (item, part ^ bit)
        return item * ray_parts + part

    def exchange(array, *partners):
        return lax.ppermute(
            array, ("items", "rays"), [(i, flip(i, partners)) for i in range(items * ray_parts)]
        )

    low_bit, high_bit = sorted((first, second))
    from_low = exchange(quarters[1], low_bit)
    from_high = exchange(quarters[2], high_bit)
    from_both = exchange(quarters[3], low_bit, high_bit)

    grad_queries, grad_keys, grad_values = run_attend_back(forward, keys, values, grad_mixture)

    held = [shape(quarter_bf16, BF16)] * 4 + [total_bf16] * 3 + [rows_bf16] * 0
    square = shape((width, width), BF16)
    held = held + [square, square, total_bf16, rows_bf16, rows_bf16, square, rows_bf16, shape((count, width), F32)]
    ray_grad, latent_grad, summed, small = pl.pallas_call(
        functools.partial(reduce_kernel, core, orders, size, script, EARLY),
        out_shape=(
            rows_bf16, shape((lat, width), BF16), shape((2, groups * size, half_width), BF16), shape((16, width), F32),
        ),
        in_specs=[anywhere()] * 15 + [vmem()] * 3,
        out_specs=[vmem(), vmem(), anywhere(), vmem()],
        scratch_shapes=[pltpu.VMEM(h.shape, h.dtype) for h in held] + [
            pltpu.VMEM((2, late_groups * size, half_width), BF16),
            pltpu.VMEM((late_groups * size, half_width), BF16),
            pltpu.VMEM((EARLY * quarter + late_groups * size, half_width), BF16),
            pltpu.VMEM((EARLY * quarter + late_groups * size, half_width), BF16),
            pltpu.VMEM((2, groups * size, half_width), BF16),
            pltpu.VMEM((bits + 2, 16, width), F32),
            pltpu.VMEM((bits + 1, 16, width), F32),
            pltpu.VMEM((4, lat, width), BF16),
            pltpu.VMEM((3, lat, width), BF16),
            pltpu.VMEM((lat, width), BF16),
            dma((15,)), dma((late_groups,)), dma((late_groups,)),
            dma((groups * bits,)), dma((groups * bits,)), dma((groups * (bits + 1),)), dma((groups * (bits + 1),)),
            dma((bits + 1,)), dma((bits + 1,)), dma((3,)), dma((3,)), dma((2 * groups,)),
        ],
        compiler_params=big(collective_id=3, has_side_effects=True),
        name="reduce",
    )(
        quarters, from_low, from_high, from_both,
        latent_normed, grad_keys, grad_values, key_weight, value_weight, latent_all,
        ray_normed, grad_queries, query_weight, x, grad_hidden,
        row(ray_gain), row(latent_gain), early_sums,
    )

    wide = shape((width, width), F32)
    step, slots = 256, 4
    down_grad, up_grad, out_grad, query_grad, key_grad, value_grad = pl.pallas_call(
        functools.partial(widen_kernel, size),
        out_shape=(shape((2 * width, width), F32), shape((width, 2 * width), F32), wide, wide, wide, wide),
        in_specs=[anywhere()],
        out_specs=[anywhere()] * 6,
        scratch_shapes=[
            pltpu.VMEM((slots, 2, step, half_width), BF16), pltpu.VMEM((slots, step, width), F32),
            dma((slots,)), dma((slots,)),
        ],
        name="widen",
    )(summed)

    return (
        ray_out[None], ray_grad[None], latent_grad[None],
        query_grad, key_grad, value_grad, out_grad, small[5],
        up_grad, small[1:3].reshape(-1), down_grad, small[0],
        small[6], small[7], small[8], small[9], small[3], small[4],
    )


def solution(mesh):
    split = P("items", "rays", None)
    in_specs = (split, split, P("items", "rays"), P("items", None), P("items", None), split) + (P(),) * 15
    out_specs = (split, split, split) + (P(),) * 15
    return jax.shard_map(
        functools.partial(on_device, mesh.shape["items"], mesh.shape["rays"]),
        mesh=mesh, in_specs=in_specs, out_specs=out_specs, check_vma=False,
    )
```

time: 350 us -> 279 us (0.80)
  Pallas kernels: 313 us -> 251 us
  other arithmetic: 19 us -> 0 us
  local copies, waits for them, and re-layouts: 17.8 us -> 22.5 us
    pallas_call x4 -> x5, Pallas kernels: 289 us -> 227 us  [the longest x1 104 us: on_device(): pl.pallas_call(functools.partial(reduce_kernel, core, orders, size, scrip...]
    slice x1 -> x0, other arithmetic: 6.88 us -> none  [part(): return summed[i * width:(i + 1) * width].astype(F32)]
    convert_element_type x1 -> x0, other arithmetic: 4.21 us -> none  [on_device(): down_grad = summed[:2 * width].astype(F32)]
  transfers between devices with their start and end apart: 0 -> 3, of which waited for: 0 -> 0; matrix products, arithmetic and copies ran while one was open for 0% -> 0% of each run, Pallas kernels for 0% -> 15%
where the time goes in v2:
time: 279 us; the launch traced here: 277 us
  Pallas kernels  251 us (90%)
  local copies, waits for them, and re-layouts  22.5 us (8%)
  starting transfers between devices  3.49 us (1%)
    pallas_call x1, Pallas kernels, on_device(): pl.pallas_call(functools.partial(reduce_kernel, core, orders, size, scrip...  104 us
    pallas_call x1, Pallas kernels, run_attend_back(): pl.pallas_call(attend_back_kernel, out_shape=(shape((count, width), BF16)...  42.6 us
    pallas_call x1, Pallas kernels, on_device(): pl.pallas_call(functools.partial(mlp_kernel, core, orders[:EARLY], size),...  38.2 us
    pallas_call x1, Pallas kernels, run_attend(): pl.pallas_call(attend_kernel, out_shape=(rows_bf16, rows_bf16, rows_bf16,...  31.6 us
    pallas_call x1, Pallas kernels, on_device(): pl.pallas_call(project_kernel, out_shape=(rows_bf16, rows_bf16, shape((pa...  23.4 us
    reshape x9, local copies, waits for them, and re-layouts, row(): return v.reshape(1, -1)  11.4 us
    pallas_call x1, Pallas kernels, on_device(): pl.pallas_call(functools.partial(widen_kernel, size), out_shape=(shape((2...  10.8 us
  transfers between devices with their start and end apart: 3, of which 0 were waited for; matrix products, arithmetic and copies ran while one was open for 0% of the time, Pallas kernels for 15%

profile of v2, /device:TPU:0, one launch (start us, length us, event | category | flops | bytes accessed | tf_op | source)
XLA Modules:
  0.0 277.4 jit_solution(4149595746753365213)
XLA Ops:
  0.7 1.3 reshape.68.ray_gain
  1.9 1.3 reshape.70.latent_gain
  3.2 1.3 reshape.72.out_bias
  4.5 1.3 reshape.74.down_bias
  5.7 1.3 reshape.69.ray_shift
  7.0 1.3 reshape.71.latent_shift
  8.3 1.3 reshape.75.mlp_gain
  9.5 1.3 reshape.76.mlp_shift
  10.8 1.3 reshape.73.up_bias
  12.1 23.4 %project.1 = (bf16[1024,768]{1,0:T(8,128)(2,1)}, bf16[1024,768]{1,0:T(8,128)(2,1)}, bf16[1408,768]{1,0:T(8,128)(2,1)}, bf16[1408,768]{1,0:T(8,128)(2,1)}, bf16[1...) custom-call(bf16[1024,768]{1,0:T(8,128)(2,1)} %bitcast.12, bf16[288,768]{1,0:T(8,128)(2,1)} %bitcast.18, ...), custom_call_target="tpu_custom_call" | custom-call | tf_op jit(solution)/shard_map/project/pallas_call | solution.py:916
  35.5 31.6 %attend.1 = (bf16[1024,768]{1,0:T(8,128)(2,1)}, bf16[1024,768]{1,0:T(8,128)(2,1)}, bf16[1024,768]{1,0:T(8,128)(2,1)}, f32[1024,128]{1,0:T(8,128)}, s32[10]{0:T(1...) custom-call(bf16[1024,768]{1,0:T(8,128)(2,1)} %get-tuple-element.49.queries, bf16[1408,768]{1,0:T(8,128)(2,1)} %get-tuple-element.50.keys, ...), custom_call_target="tpu_custom_call" | custom-call | tf_op jit(solution)/shard_map/attend/pallas_call | solution.py:383
  67.1 38.2 %mlp.1 = (bf16[1024,768]{1,0:T(8,128)(2,1)}, bf16[1024,768]{1,0:T(8,128)(2,1)}, f32[1024,768]{1,0:T(8,128)}, bf16[4,5,192,384]{3,2,1,0:T(8,128)(2,1)}, f32[8,768]{1,0:T(8,128)}) custom-call(bf16[1024,768]{1,0:T(8,128)(2,1)} %bitcast.13, bf16[1024,768]{1,0:T(8,128)(2,1)} %get-tuple-element.52.mixture, bf16[1024,768]{1,0:T(8,128)(2,1)} %bitcast.17, ...), custom_call_target="tpu_custom_call" | custom-call | tf_op jit(solution)/shard_map/mlp/pallas_call | solution.py:944
  105.4 2.7 slice_bitcast_fusion
  108.0 0.4 collective-permute-start.2
  108.4 2.6 collective-permute-start.1
  111.0 0.5 collective-permute-start
  111.5 42.6 %attend_back.1 = (bf16[1024,768]{1,0:T(8,128)(2,1)}, bf16[1152,768]{1,0:T(8,128)(2,1)}, bf16[1152,768]{1,0:T(8,128)(2,1)}) custom-call(s32[10]{0:T(128)} %get-tuple-element.56.meta, bf16[1024,768]{1,0:T(8,128)(2,1)} %get-tuple-element.57.sorted_queries, bf16[1408,768]{1,0:T(8,128)(2,1)} %get-tuple-element.50.keys, ...), custom_call_target="tpu_custom_call" | custom-call | tf_op jit(solution)/shard_map/attend_back/pallas_call | solution.py:413
  154.1 0.0 collective-permute-done.2.from_both
  154.1 0.0 copy-start.2
  154.1 0.0 collective-permute-done.1.from_second
  154.2 0.0 copy-start.3
  154.2 0.0 collective-permute-done.from_first
  154.2 0.0 copy-start.4
  154.2 0.8 copy-done.2
  155.0 0.2 copy-done.3
  155.2 0.2 copy-done.4
  155.5 103.9 %reduce.17 = (bf16[1024,768]{1,0:T(8,128)(2,1)}, bf16[288,768]{1,0:T(8,128)(2,1)}, bf16[2,6144,384]{2,1,0:T(8,128)(2,1)}, f32[16,768]{1,0:T(8,128)}) custom-call(bf16[4,5,192,384]{3,2,1,0:T(8,128)(2,1)} %get-tuple-element.54.quarters, bf16[5,192,384]{2,1,0:T(8,128)(2,1)} %copy-done.4, bf16[5,192,384]{2,1,0:T(8,128)(2,1)} %copy-done.3, ...), custom_call_target="tpu_custom_call" | custom-call | tf_op jit(solution)/shard_map/reduce/pallas_call | solution.py:985
  259.4 0.7 slice.40
  260.2 1.8 slice_reduce_fusion
  261.9 0.6 reshape.77
  262.5 0.0 copy-start
  262.5 10.8 %widen.1 = (f32[1536,768]{1,0:T(8,128)}, f32[768,1536]{1,0:T(8,128)}, f32[768,768]{1,0:T(8,128)}, f32[768,768]{1,0:T(8,128)}, f32[768,768]{1,0:T(8,128)}, /*index=5*/f32[768,768]{1,0:T(8,128)}) custom-call(bf16[2,6144,384]{2,1,0:T(8,128)(2,1)} %get-tuple-element.72.summed), custom_call_target="tpu_custom_call" | custom-call | tf_op jit(solution)/shard_map/widen/pallas_call | solution.py:1018
  273.3 0.0 copy-start.1
  273.4 0.0 copy-done
  273.4 1.1 copy.42
  274.5 0.8 copy-done.1
  275.3 0.0 copy-start.5
  275.3 1.1 copy.43
  276.5 0.2 copy-done.5
  276.6 0.8 copy.44
Async XLA Ops:
  108.0 46.1 %collective-permute-start.2 = (bf16[5,192,384]{2,1,0:T(8,128)(2,1)}, bf16[5,192,384]{2,1,0:T(8,128)(2,1)S(1)}, u32[]{:S(2)}, u32[]{:S(2)}) collective-permute-start(bf16[5,192,384]{2,1,0:T(8,128)(2,1)} %get-tuple-element.88), channel_id=1, source_target_pairs={{0,6},{1,7},{2,4},{3,5},{4,2},{5,3},{6,0},{7,1},{8,14},{9,15},{10,... | collective-permute-start | bytes 2211848 | tf_op jit(solution)/shard_map/ppermute | solution.py:971
  108.4 45.7 %collective-permute-start.1 = (bf16[5,192,384]{2,1,0:T(8,128)(2,1)S(1)}, bf16[5,192,384]{2,1,0:T(8,128)(2,1)S(1)}, u32[]{:S(2)}, u32[]{:S(2)}) collective-permute-start(bf16[5,192,384]{2,1,0:T(8,128)(2,1)S(1)} %get-tuple-element.89), channel_id=1, source_target_pairs={{0,2},{1,3},{2,0},{3,1},{4,6},{5,7},{6,4},{7,5},{8,10},{9,11},{10,... | collective-permute-start | bytes 2211848 | tf_op jit(solution)/shard_map/ppermute | solution.py:971
  111.0 43.2 %collective-permute-start = (bf16[5,192,384]{2,1,0:T(8,128)(2,1)S(1)}, bf16[5,192,384]{2,1,0:T(8,128)(2,1)S(1)}, u32[]{:S(2)}, u32[]{:S(2)}) collective-permute-start(bf16[5,192,384]{2,1,0:T(8,128)(2,1)S(1)} %get-tuple-element.90), channel_id=1, source_target_pairs={{0,4},{1,5},{2,6},{3,7},{4,0},{5,1},{6,2},{7,3},{8,12},{9,13},{10,... | collective-permute-start | bytes 2211848 | tf_op jit(solution)/shard_map/ppermute | solution.py:971
  154.1 0.9 copy-start.2
  154.2 1.1 copy-start.3
  154.2 1.3 copy-start.4
  262.5 10.8 %copy-start = (bf16[1024,768]{1,0:T(8,128)(2,1)S(1)}, bf16[1024,768]{1,0:T(8,128)(2,1)}, u32[]{:S(2)}) copy-start(bf16[1024,768]{1,0:T(8,128)(2,1)} %get-tuple-element.53) | copy-start | bytes 4718596
  273.3 2.0 copy-start.1
  275.3 1.3 copy-start.5

commit v3 on v2

--- a/solution.py
+++ b/solution.py
@@ -43,6 +43,10 @@
     )
 
 
+def as_row(vector):
+    return vector[...].reshape(1, -1)
+
+
 def vmem():
     return pl.BlockSpec(memory_space=pltpu.VMEM)
 
@@ -97,7 +101,7 @@
     def _(i):
         rows = pl.ds(pl.multiple_of(i * chunk, chunk), chunk)
         standard, _ = stand(rays[rows, :].astype(F32))
-        normed = (standard * ray_gain[...] + ray_shift[...]).astype(BF16)
+        normed = (standard * as_row(ray_gain) + as_row(ray_shift)).astype(BF16)
         ray_normed[rows, :] = normed
         projected = dot(normed, query_w[...]).astype(BF16)
         queries[rows, :] = (projected.astype(F32) * SCALE).astype(BF16)
@@ -106,7 +110,7 @@
         rows = pl.ds(pl.multiple_of(owner * lat, 32), lat)
         latent_all[rows, :] = raw
         standard, _ = stand(raw.astype(F32))
-        normed = (standard * latent_gain[...] + latent_shift[...]).astype(BF16)
+        normed = (standard * as_row(latent_gain) + as_row(latent_shift)).astype(BF16)
         latent_normed[rows, :] = normed
         keys[rows, :] = dot(normed, key_w[...]).astype(BF16)
         values[rows, :] = dot(normed, value_w[...]).astype(BF16)
@@ -442,20 +446,16 @@
     )
 
 
-def part_start(order, size, flipped=()):
-    start = 0
-    for i, partner in enumerate(order[:2]):
-        mine = bit_of(partner)
-        if partner in flipped:
-            mine = 1 - mine
-        start = start + mine * (size >> (i + 1))
-    return start
+def quarter_start(first, second, size, flips):
+    one = bit_of(first) if not flips[0] else 1 - bit_of(first)
+    two = bit_of(second) if not flips[1] else 1 - bit_of(second)
+    return one * (size // 2) + two * (size // 4)
 
 
 def mlp_kernel(
-    core, orders, size,
+    core, first, second, size,
     rays, mixture, cotangent, out_w, up_w, down_w, out_bias, up_bias, down_bias, mlp_gain, mlp_shift,
-    ray_out, grad_mixture, grad_hidden, quarters, sums,
+    ray_out, grad_mixture, grad_hidden, kept, to_first, to_second, to_both, sums,
     act, grad_pre, normed, branch, early, landed, send_sem, recv_sem,
 ):
     chunk = 256
@@ -470,17 +470,17 @@
     @pl.loop(0, rays.shape[0] // chunk)
     def _(i):
         rows = pl.ds(pl.multiple_of(i * chunk, chunk), chunk)
-        hidden = rays[rows, :].astype(F32) + dot(mixture[rows, :], out_w[...]) + out_bias[...]
+        hidden = rays[rows, :].astype(F32) + dot(mixture[rows, :], out_w[...]) + as_row(out_bias)
         standard, inverse = stand(hidden)
-        low = (standard * mlp_gain[...] + mlp_shift[...]).astype(BF16)
+        low = (standard * as_row(mlp_gain) + as_row(mlp_shift)).astype(BF16)
         normed[rows, :] = low
         upstream = cotangent[rows, :]
         half = 768
-        out = hidden + down_bias[...]
+        out = hidden + as_row(down_bias)
         grad_mlp = jnp.zeros((chunk, width), F32)
         for j in range(up_w.shape[1] // half):
             cols = slice(j * half, (j + 1) * half)
-            pre = dot(low, up_w[:, cols]) + up_bias[:, cols]
+            pre = dot(low, up_w[:, cols]) + up_bias[cols].reshape(1, half)
             square = pre * pre
             bend = jnp.tanh(root * pre * (1.0 + cubic * square))
             rise = 0.5 * (1.0 + bend)
@@ -497,7 +497,7 @@
         sums[0:1, :] += jnp.sum(wide, axis=0, keepdims=True)
         sums[3:4, :] += jnp.sum(grad_mlp * standard, axis=0, keepdims=True)
         sums[4:5, :] += jnp.sum(grad_mlp, axis=0, keepdims=True)
-        through = wide + norm_back(grad_mlp, standard, inverse, mlp_gain[...])
+        through = wide + norm_back(grad_mlp, standard, inverse, as_row(mlp_gain))
         grad_hidden[rows, :] = through
         rounded = through.astype(BF16)
         branch[rows, :] = rounded
@@ -538,12 +538,10 @@
         swap(tile).wait_recv()
 
     quarter = size // 4
-    for g, order in enumerate(orders):
-        first, second = sorted(order[:2])
-        for target, flipped in enumerate(((), (first,), (second,), (first, second))):
-            start = pl.multiple_of(g * size + part_start(order, size, flipped), 16)
-            rows = pl.ds(start, quarter)
-            quarters[target, g] = (early[mine, rows, :].astype(F32) + landed[rows, :].astype(F32)).astype(BF16)
+    for g in range(EARLY):
+        for target, flips in ((kept, (0, 0)), (to_first, (1, 0)), (to_second, (0, 1)), (to_both, (1, 1))):
+            rows = pl.ds(pl.multiple_of(g * size + quarter_start(first, second, size, flips), 16), quarter)
+            target[g] = (early[mine, rows, :].astype(F32) + landed[rows, :].astype(F32)).astype(BF16)
 
     @pl.loop(0, 5 * tiles)
     def _(tile):
@@ -551,32 +549,32 @@
 
 
 def reduce_kernel(
-    core, orders, size, script, early_groups,
-    quarters, from_first, from_second, from_both,
+    core, bits, halvings, doublings, size, script,
+    kept, from_first, from_second, from_both,
     latent_normed, grad_keys, grad_values, key_w, value_w, latent_all,
     ray_normed, grad_queries, query_w, rays, grad_hidden,
     ray_gain, latent_gain, early_sums,
     ray_grad, latent_grad, summed, small,
-    v_quarters, v_first, v_second, v_both,
+    v_kept, v_first, v_second, v_both,
     v_latent_normed, v_grad_keys, v_grad_values, v_key_w, v_value_w, v_latent_all,
     v_ray_normed, v_grad_queries, v_query_w, v_rays, v_grad_hidden,
-    late, late_landed, acc, landed, gathered,
+    late, late_landed, early_acc, early_landed, late_acc, late_in, gathered,
     smalls, small_landed, latent_part, latent_landed, latent_mid,
     load_sem, swap_send, swap_recv, send_sem, recv_sem, back_send, back_recv,
     small_send, small_recv, latent_send, latent_recv, store_sem,
 ):
-    bits = len(orders[0])
-    partners = sorted(orders[0] + (core,))
+    count = len(bits)
+    partners = sorted(bits + (core,))
     width = rays.shape[1]
     half_width = width // 2
-    quarter = size // 4
+    piece = size >> count
     held = (
-        v_quarters, v_first, v_second, v_both,
+        v_kept, v_first, v_second, v_both,
         v_latent_normed, v_grad_keys, v_grad_values, v_key_w, v_value_w, v_latent_all,
         v_ray_normed, v_grad_queries, v_query_w, v_rays, v_grad_hidden,
     )
     given = (
-        quarters.at[0], from_first, from_second, from_both,
+        kept, from_first, from_second, from_both,
         latent_normed, grad_keys, grad_values, key_w, value_w, latent_all,
         ray_normed, grad_queries, query_w, rays, grad_hidden,
     )
@@ -587,8 +585,8 @@
     mine = bit_of(core)
     loaded = [0]
 
-    def need(count):
-        while loaded[0] < count:
+    def need(last):
+        while loaded[0] < last:
             loads[loaded[0]].wait()
             loaded[0] += 1
 
@@ -600,100 +598,99 @@
         pass
 
     groups = []
-    for g, order in enumerate(orders):
+    for g in range(EARLY + late_landed.shape[0] // size):
         group = Group()
-        group.order, group.start, group.size, group.step, group.starts, group.live = order, g * size, size, 0, [], None
-        group.index, group.at, group.shift = g, 0, early_groups * (size - quarter)
+        group.index, group.at, group.live = g, 0, None
+        group.early = g < EARLY
+        group.free = list(bits[2:] if group.early else bits)
+        group.halvings, group.doublings = list(halvings[g]), list(doublings[g])
+        group.done = []
+        group.acc = early_acc.at[g] if group.early else late_acc.at[g - EARLY]
+        group.landed = early_landed.at[g] if group.early else late_in.at[g - EARLY]
         groups.append(group)
 
-    def rows_at(start, count):
-        return pl.ds(pl.multiple_of(start, 16), count)
-
-    def add_rows(target, there, first, second, here, count):
-        tile = next(t for t in (64, 48, 32, 16) if count % t == 0)
-
-        @pl.loop(0, count // tile)
-        def _(i):
-            one = first[rows_at(here[0] + i * tile, tile), :].astype(F32)
-            two = second[rows_at(here[1] + i * tile, tile), :].astype(F32)
-            target[rows_at(there + i * tile, tile), :] = (one + two).astype(BF16)
+    def combos(names):
+        for i in range(1 << len(names)):
+            yield {name: (i >> k) & 1 for k, name in enumerate(names)}
+
+    def dims(group):
+        return bits[2:] if group.early else bits
 
     def swap_begin(group):
-        rows = rows_at((group.index - early_groups) * size, size)
-        i = group.index - early_groups
+        i = group.index - EARLY
+        rows = pl.ds(i * size, size)
         group.live = remote(late.at[1 - mine, rows], late_landed.at[rows], swap_send.at[i], swap_recv.at[i], core)
         group.live.start()
 
     def swap_finish(group):
         group.live.wait_recv()
-        base = (group.index - early_groups) * size
-        add_rows(acc, group.start - group.shift, late.at[mine], late_landed, (base, base), size)
+        base = (group.index - EARLY) * size
+        for i in range(1 << count):
+            rows = slice(base + i * piece, base + (i + 1) * piece)
+            total = late[mine, rows, :].astype(F32) + late_landed[rows, :].astype(F32)
+            group.acc[tuple((i >> (count - 1 - k)) & 1 for k in range(count))] = total.astype(BF16)
         group.live.wait_send()
 
     def halve_begin(group):
-        partner = group.order[group.step]
-        half = group.size // 2
-        bit = bit_of(partner)
-        give, keep = group.start + (1 - bit) * half, group.start + bit * half
-        if group.index < early_groups:
-            slot = (group.index + 1) * quarter - group.size
-        else:
-            slot = early_groups * quarter + (group.index - early_groups + 1) * size - group.size
-        i = group.index * bits + group.step
-        copy = remote(
-            acc.at[rows_at(give - group.shift, half)], landed.at[rows_at(slot, half)], send_sem.at[i], recv_sem.at[i], partner
-        )
-        copy.start()
-        group.starts.append(group.start)
-        group.live = (copy, keep, slot, half)
+        bit = group.halvings[len(group.done)]
+        i = group.index * count + len(group.done)
+
+        def at(value):
+            return tuple(
+                pl.ds(value, 1) if d == bit else pl.ds(bit_of(d), 1) if d in group.done else slice(None)
+                for d in dims(group)
+            )
+
+        own = bit_of(bit)
+        group.live = remote(group.acc.at[at(1 - own)], group.landed.at[at(own)], send_sem.at[i], recv_sem.at[i], bit)
+        group.live.start()
 
     def halve_finish(group):
-        copy, keep, slot, half = group.live
-        copy.wait_recv()
-        last = group.step == bits - 1
-        here = keep - group.shift
-        add_rows(gathered.at[mine] if last else acc, keep if last else here, acc, landed, (here, slot), half)
-        copy.wait_send()
-        group.start, group.size = keep, half
+        bit = group.halvings[len(group.done)]
+        group.live.wait_recv()
+        own = bit_of(bit)
+        group.done.append(bit)
+        last = len(group.done) == len(dims(group))
+        for combo in combos([d for d in dims(group) if d not in group.done]):
+            keep = tuple(combo[d] if d in combo else bit_of(d) for d in dims(group))
+            there = tuple(1 - own if d == bit else k for d, k in zip(dims(group), keep))
+            total = (group.acc[keep].astype(F32) + group.landed[there].astype(F32)).astype(BF16)
+            if last:
+                gathered[(mine, group.index) + tuple(bit_of(d) for d in bits)] = total
+            else:
+                group.acc[keep] = total
+        group.live.wait_send()
+
+    def double_begin(group):
+        done = group.doublings[: group.step]
+        bit = group.doublings[group.step] if group.step < count else core
+        i = group.index * (count + 1) + group.step
+        part = gathered.at[
+            (mine, group.index) + tuple(slice(None) if d in done else pl.ds(bit_of(d), 1) for d in bits)
+        ]
+        group.live = remote(part, part, back_send.at[i], back_recv.at[i], bit)
+        group.live.start()
         group.step += 1
-
-    def double_begin(group):
-        rows = rows_at(group.start, group.size)
-        step = group.step - 1
-        i = group.index * (bits + 1) + step + 1
-        partner = group.order[step] if step >= 0 else core
-        piece = gathered.at[mine, rows]
-        group.live = remote(piece, piece, back_send.at[i], back_recv.at[i], partner)
-        group.live.start()
 
     def double_finish(group):
         group.live.wait_recv()
         group.live.wait_send()
-        group.step -= 1
-        if group.step >= 0:
-            group.start = group.starts[group.step]
-            group.size *= 2
 
     stores = []
 
     def store(group):
-        rows = pl.ds(group.index * size, size)
         for side in range(2):
             copy = pltpu.make_async_copy(
-                gathered.at[side, rows], summed.at[side, rows], store_sem.at[2 * group.index + side]
+                gathered.at[side, group.index], summed.at[side, group.index], store_sem.at[2 * group.index + side]
             )
             copy.start()
             stores.append(copy)
 
     def plan(group):
-        steps = []
-        halvings = bits
-        if group.index < early_groups:
-            halvings = bits - 2
-        else:
-            steps.append((swap_begin, swap_finish))
-        steps += [(halve_begin, halve_finish)] * halvings
-        steps += [(double_begin, double_finish)] * (bits + 1)
+        group.step = 0
+        steps = [] if group.early else [(swap_begin, swap_finish)]
+        steps += [(halve_begin, halve_finish)] * len(group.halvings)
+        steps += [(double_begin, double_finish)] * (count + 1)
         return steps
 
     plans = [plan(group) for group in groups]
@@ -719,20 +716,18 @@
     far_copy = remote(latent_mid, latent_landed.at[2], latent_send.at[2], latent_recv.at[2], far)
     small_copies = [
         remote(smalls.at[t], small_landed.at[t], small_send.at[t], small_recv.at[t], partners[t])
-        for t in range(bits + 1)
+        for t in range(count + 1)
     ]
 
     def early_begin():
         need(4)
-        for g in range(early_groups):
-            group = groups[g]
-            start = g * size
-            for i, partner in enumerate(group.order[:2]):
-                group.starts.append(start)
-                start = start + bit_of(partner) * (size >> (i + 1))
-            group.start, group.size, group.step, group.shift = start, quarter, 2, start - g * quarter
-            total = v_quarters[g].astype(F32) + v_first[g].astype(F32) + v_second[g].astype(F32) + v_both[g].astype(F32)
-            acc[pl.ds(g * quarter, quarter), :] = total.astype(BF16)
+        for g in range(EARLY):
+            for i in range(1 << (count - 2)):
+                rows = slice(i * piece, (i + 1) * piece)
+                total = v_kept[g, rows, :].astype(F32)
+                for other in (v_first, v_second, v_both):
+                    total = total + other[g, rows, :].astype(F32)
+                early_acc[(g,) + tuple((i >> (count - 3 - k)) & 1 for k in range(count - 2))] = total.astype(BF16)
             advance(g)
 
     step = 256
@@ -746,7 +741,7 @@
             late[0, rows, :] = part[:, :half_width]
             late[1, rows, :] = part[:, half_width:]
 
-        advance(early_groups + index)
+        advance(EARLY + index)
 
     def query_part():
         need(12)
@@ -789,7 +784,7 @@
             latent_part[me].astype(F32) + latent_landed[lax.div(me, 2)].astype(F32) + latent_landed[2].astype(F32)
         )
         standard, inverse = stand(v_latent_all[pl.ds(pl.multiple_of(me * lat, 32), lat), :].astype(F32))
-        latent_grad[...] = norm_back(grad_normed, standard, inverse, latent_gain[...]).astype(BF16)
+        latent_grad[...] = norm_back(grad_normed, standard, inverse, as_row(latent_gain)).astype(BF16)
 
     def rays_part():
         need(15)
@@ -803,7 +798,7 @@
             smalls[0, 6:7, :] += jnp.sum(grad_normed * standard, axis=0, keepdims=True)
             smalls[0, 7:8, :] += jnp.sum(grad_normed, axis=0, keepdims=True)
             ray_grad[rows, :] = (
-                v_grad_hidden[rows, :] + norm_back(grad_normed, standard, inverse, ray_gain[...])
+                v_grad_hidden[rows, :] + norm_back(grad_normed, standard, inverse, as_row(ray_gain))
             ).astype(BF16)
 
         small_copies[0].start()
@@ -816,10 +811,10 @@
         smalls[t + 1] = smalls[t] + small_landed[t]
         small_copies[t].wait_send()
         small_at[0] += 1
-        if t + 1 <= bits:
+        if t + 1 <= count:
             small_copies[t + 1].start()
         else:
-            small[...] = smalls[bits + 1]
+            small[...] = smalls[count + 1]
 
     tasks = {
         "E": early_begin, "Q": query_part, "K": key_part, "V": value_part, "L": latents_begin, "M": latents_next,
@@ -830,7 +825,7 @@
             tasks[letter]()
         else:
             advance(int(letter))
-    while small_at[0] <= bits:
+    while small_at[0] <= count:
         small_next()
     while any(group.at <= len(steps) for group, steps in zip(groups, plans)):
         for g in range(len(groups)):
@@ -840,8 +835,13 @@
         copy.wait()
 
 
-def widen_kernel(size, summed, *refs):
-    down, up, out, query, key, value, held, wide, load_sem, store_sem = refs
+def widen_kernel(size, summed, small, *refs):
+    down, up, out, query, key, value = refs[:6]
+    vectors, up_bias, (held, wide, load_sem, store_sem) = refs[6:14], refs[14], refs[15:]
+    for at, vector in zip((5, 0, 6, 7, 8, 9, 3, 4), vectors):
+        vector[...] = small[at]
+    up_bias[: small.shape[1]] = small[1]
+    up_bias[small.shape[1] :] = small[2]
     width = held.shape[3] * 2
     half = width // 2
     step = held.shape[2]
@@ -881,14 +881,25 @@
 EARLY = 5
 
 
+HALVINGS = ("wz", "zw", "zw", "wz", "zw", "yxzw", "zxyw", "yxwz")
+DOUBLINGS = ("wzxy", "zwyx", "wzyx", "wyxz", "wzyx", "xwyz", "zwyx", "xzwy")
+SCRIPT = (
+    "EQKV01526L7340125RM63547S012S365S407S12NS5304657",
+    "163726517031467032562475465767",
+)
+
+
 def ways(items, ray_parts):
     core, y, x = ("rays", 1), ("rays", 2), ("items", 1)
-    others = tuple(("items", 2 << i) for i in range(log2(items) - 1)) + tuple(
+    bits = (x, y) + tuple(("items", 2 << i) for i in range(log2(items) - 1)) + tuple(
         ("rays", 4 << i) for i in range(log2(ray_parts) - 2)
     )
-    a, b, c, d = (x, y) + others, (y, x) + others, (x, y) + others[::-1], (y, x) + others[::-1]
-    orders = (a, d, b, c, a, d, a, c)
-    return core, x, y, orders, "EKVQL0126M73451RN0S27615S4036S1275S04S"
+    if len(bits) != 4:
+        return core, bits, (bits[2:],) * EARLY + (bits,) * 3, (bits[::-1],) * (EARLY + 3), "EKQVLRMN"
+    name = dict(zip("xyzw", bits))
+    halvings = tuple(tuple(name[c] for c in word) for word in HALVINGS)
+    doublings = tuple(tuple(name[c] for c in word) for word in DOUBLINGS)
+    return core, bits, halvings, doublings, "".join(SCRIPT)
 
 
 def on_device(
@@ -905,9 +916,6 @@
     x = rays[0]
     upstream = cotangent[0]
 
-    def row(v):
-        return v.reshape(1, -1)
-
     shape = jax.ShapeDtypeStruct
     rows_bf16 = shape((count, width), BF16)
     total_bf16 = shape((total, width), BF16)
@@ -925,29 +933,33 @@
         name="project",
     )(
         x, latents[0], query_weight, key_weight, value_weight,
-        row(ray_gain), row(ray_shift), row(latent_gain), row(latent_shift),
+        ray_gain, ray_shift, latent_gain, latent_shift,
     )
 
     forward = run_attend(queries, keys, values, ray_scene, latent_scene, latent_pad)
     mixture = forward[0]
 
-    core, first, second, orders, script = ways(items, ray_parts)
-    bits = len(orders[0])
-    unit = 16 << bits
+    core, bits, halvings, doublings, script = ways(items, ray_parts)
+    first, second = bits[:2]
+    nbits = len(bits)
+    unit = 16 << nbits
     size = (width + unit - 1) // unit * unit
     quarter = size // 4
     half_width = width // 2
-    groups = len(orders)
+    groups = len(halvings)
     late_groups = groups - EARLY
+    piece = (size >> nbits, half_width)
     quarter_bf16 = (EARLY, quarter, half_width)
 
-    ray_out, grad_mixture, grad_hidden, quarters, early_sums = pl.pallas_call(
-        functools.partial(mlp_kernel, core, orders[:EARLY], size),
+    ray_out, grad_mixture, grad_hidden, kept, to_first, to_second, to_both, early_sums = pl.pallas_call(
+        functools.partial(mlp_kernel, core, first, second, size),
         out_shape=(
-            rows_bf16, rows_bf16, shape((count, width), F32), shape((4,) + quarter_bf16, BF16), shape((8, width), F32),
+            rows_bf16, rows_bf16, shape((count, width), F32),
+            shape(quarter_bf16, BF16), shape(quarter_bf16, BF16), shape(quarter_bf16, BF16), shape(quarter_bf16, BF16),
+            shape((8, width), F32),
         ),
         in_specs=[vmem()] * 11,
-        out_specs=[vmem()] * 5,
+        out_specs=[vmem()] * 8,
         scratch_shapes=[
             pltpu.VMEM((count, hidden_width), BF16), pltpu.VMEM((count, hidden_width), BF16),
             pltpu.VMEM((count, width), BF16), pltpu.VMEM((count, width), BF16),
@@ -958,7 +970,7 @@
         name="mlp",
     )(
         x, mixture, upstream, out_weight, up_weight, down_weight,
-        row(out_bias), row(up_bias), row(down_bias), row(mlp_gain), row(mlp_shift),
+        out_bias, up_bias, down_bias, mlp_gain, mlp_shift,
     )
 
     def flip(index, partners):
@@ -972,10 +984,9 @@
             array, ("items", "rays"), [(i, flip(i, partners)) for i in range(items * ray_parts)]
         )
 
-    low_bit, high_bit = sorted((first, second))
-    from_low = exchange(quarters[1], low_bit)
-    from_high = exchange(quarters[2], high_bit)
-    from_both = exchange(quarters[3], low_bit, high_bit)
+    from_first = exchange(to_first, first)
+    from_second = exchange(to_second, second)
+    from_both = exchange(to_both, first, second)
 
     grad_queries, grad_keys, grad_values = run_attend_back(forward, keys, values, grad_mixture)
 
@@ -983,55 +994,63 @@
     square = shape((width, width), BF16)
     held = held + [square, square, total_bf16, rows_bf16, rows_bf16, square, rows_bf16, shape((count, width), F32)]
     ray_grad, latent_grad, summed, small = pl.pallas_call(
-        functools.partial(reduce_kernel, core, orders, size, script, EARLY),
+        functools.partial(reduce_kernel, core, bits, halvings, doublings, size, script),
         out_shape=(
-            rows_bf16, shape((lat, width), BF16), shape((2, groups * size, half_width), BF16), shape((16, width), F32),
+            rows_bf16, shape((lat, width), BF16), shape((2, groups) + (2,) * nbits + piece, BF16),
+            shape((16, width), F32),
         ),
         in_specs=[anywhere()] * 15 + [vmem()] * 3,
         out_specs=[vmem(), vmem(), anywhere(), vmem()],
         scratch_shapes=[pltpu.VMEM(h.shape, h.dtype) for h in held] + [
             pltpu.VMEM((2, late_groups * size, half_width), BF16),
             pltpu.VMEM((late_groups * size, half_width), BF16),
-            pltpu.VMEM((EARLY * quarter + late_groups * size, half_width), BF16),
-            pltpu.VMEM((EARLY * quarter + late_groups * size, half_width), BF16),
-            pltpu.VMEM((2, groups * size, half_width), BF16),
-            pltpu.VMEM((bits + 2, 16, width), F32),
-            pltpu.VMEM((bits + 1, 16, width), F32),
+            pltpu.VMEM((EARLY,) + (2,) * (nbits - 2) + piece, BF16),
+            pltpu.VMEM((EARLY,) + (2,) * (nbits - 2) + piece, BF16),
+            pltpu.VMEM((late_groups,) + (2,) * nbits + piece, BF16),
+            pltpu.VMEM((late_groups,) + (2,) * nbits + piece, BF16),
+            pltpu.VMEM((2, groups) + (2,) * nbits + piece, BF16),
+            pltpu.VMEM((nbits + 2, 16, width), F32),
+            pltpu.VMEM((nbits + 1, 16, width), F32),
             pltpu.VMEM((4, lat, width), BF16),
             pltpu.VMEM((3, lat, width), BF16),
             pltpu.VMEM((lat, width), BF16),
             dma((15,)), dma((late_groups,)), dma((late_groups,)),
-            dma((groups * bits,)), dma((groups * bits,)), dma((groups * (bits + 1),)), dma((groups * (bits + 1),)),
-            dma((bits + 1,)), dma((bits + 1,)), dma((3,)), dma((3,)), dma((2 * groups,)),
+            dma((groups * nbits,)), dma((groups * nbits,)), dma((groups * (nbits + 1),)), dma((groups * (nbits + 1),)),
+            dma((nbits + 1,)), dma((nbits + 1,)), dma((3,)), dma((3,)), dma((2 * groups,)),
         ],
         compiler_params=big(collective_id=3, has_side_effects=True),
         name="reduce",
     )(
-        quarters, from_low, from_high, from_both,
+        kept, from_first, from_second, from_both,
         latent_normed, grad_keys, grad_values, key_weight, value_weight, latent_all,
         ray_normed, grad_queries, query_weight, x, grad_hidden,
-        row(ray_gain), row(latent_gain), early_sums,
+        ray_gain, latent_gain, early_sums,
     )
 
     wide = shape((width, width), F32)
     step, slots = 256, 4
-    down_grad, up_grad, out_grad, query_grad, key_grad, value_grad = pl.pallas_call(
+    (
+        down_grad, up_grad, out_grad, query_grad, key_grad, value_grad,
+        out_bias_grad, down_bias_grad, ray_gain_grad, ray_shift_grad, latent_gain_grad, latent_shift_grad,
+        mlp_gain_grad, mlp_shift_grad, up_bias_grad,
+    ) = pl.pallas_call(
         functools.partial(widen_kernel, size),
-        out_shape=(shape((2 * width, width), F32), shape((width, 2 * width), F32), wide, wide, wide, wide),
-        in_specs=[anywhere()],
-        out_specs=[anywhere()] * 6,
+        out_shape=(shape((2 * width, width), F32), shape((width, 2 * width), F32), wide, wide, wide, wide)
+        + (shape((width,), F32),) * 8 + (shape((hidden_width,), F32),),
+        in_specs=[anywhere(), vmem()],
+        out_specs=[anywhere()] * 6 + [vmem()] * 9,
         scratch_shapes=[
             pltpu.VMEM((slots, 2, step, half_width), BF16), pltpu.VMEM((slots, step, width), F32),
             dma((slots,)), dma((slots,)),
         ],
         name="widen",
-    )(summed)
+    )(summed.reshape(2, groups * size, half_width), small)
 
     return (
         ray_out[None], ray_grad[None], latent_grad[None],
-        query_grad, key_grad, value_grad, out_grad, small[5],
-        up_grad, small[1:3].reshape(-1), down_grad, small[0],
-        small[6], small[7], small[8], small[9], small[3], small[4],
+        query_grad, key_grad, value_grad, out_grad, out_bias_grad,
+        up_grad, up_bias_grad, down_grad, down_bias_grad,
+        ray_gain_grad, ray_shift_grad, latent_gain_grad, latent_shift_grad, mlp_gain_grad, mlp_shift_grad,
     )
 
 

time: 279 us -> 245 us (0.88)
  Pallas kernels: 251 us -> 233 us
  local copies, waits for them, and re-layouts: 22.5 us -> 5.34 us
    pallas_call x2, Pallas kernels: 142 us -> 123 us  [the longest x1 84.5 us: on_device(): pl.pallas_call(functools.partial(reduce_kernel, core, bits, halvings, dou...]
    reshape x10 -> x0, local copies, waits for them, and re-layouts: 12 us -> none  [the longest x9 11.4 us: row(): return v.reshape(1, -1)]
  transfers between devices with their start and end apart: 3 -> 3, of which waited for: 0 -> 0; matrix products, arithmetic and copies ran while one was open for 0% -> 0% of each run, Pallas kernels for 15% -> 18%
where the time goes in v3:
time: 245 us; the launch traced here: 244 us
  Pallas kernels  233 us (95%)
  local copies, waits for them, and re-layouts  5.34 us (2%)
  starting transfers between devices  4.51 us (2%)
    pallas_call x1, Pallas kernels, on_device(): pl.pallas_call(functools.partial(reduce_kernel, core, bits, halvings, dou...  84.5 us
    pallas_call x1, Pallas kernels, run_attend_back(): pl.pallas_call(attend_back_kernel, out_shape=(shape((count, width), BF16)...  42.8 us
    pallas_call x1, Pallas kernels, on_device(): pl.pallas_call(functools.partial(mlp_kernel, core, first, second, size),...  38.3 us
    pallas_call x1, Pallas kernels, run_attend(): pl.pallas_call(attend_kernel, out_shape=(rows_bf16, rows_bf16, rows_bf16,...  31.7 us
    pallas_call x1, Pallas kernels, on_device(): pl.pallas_call(project_kernel, out_shape=(rows_bf16, rows_bf16, shape((pa...  23.5 us
    pallas_call x1, Pallas kernels, on_device(): pl.pallas_call(functools.partial(widen_kernel, size), out_shape=(shape((2...  12.2 us
    unnamed x15, local copies, waits for them, and re-layouts  5.34 us
  transfers between devices with their start and end apart: 3, of which 0 were waited for; matrix products, arithmetic and copies ran while one was open for 0% of the time, Pallas kernels for 18%

profile of v3, /device:TPU:0, one launch (start us, length us, event | category | flops | bytes accessed | tf_op | source)
XLA Modules:
  0.0 243.7 jit_solution(5238319984011543426)
XLA Ops:
  0.7 23.5 %project.1 = (bf16[1024,768]{1,0:T(8,128)(2,1)}, bf16[1024,768]{1,0:T(8,128)(2,1)}, bf16[1408,768]{1,0:T(8,128)(2,1)}, bf16[1408,768]{1,0:T(8,128)(2,1)}, bf16[1...) custom-call(bf16[1024,768]{1,0:T(8,128)(2,1)} %bitcast.7, bf16[288,768]{1,0:T(8,128)(2,1)} %bitcast.15, ...), custom_call_target="tpu_custom_call" | custom-call | tf_op jit(solution)/shard_map/project/pallas_call | solution.py:924
  24.2 31.7 %attend.1 = (bf16[1024,768]{1,0:T(8,128)(2,1)}, bf16[1024,768]{1,0:T(8,128)(2,1)}, bf16[1024,768]{1,0:T(8,128)(2,1)}, f32[1024,128]{1,0:T(8,128)}, s32[10]{0:T(1...) custom-call(bf16[1024,768]{1,0:T(8,128)(2,1)} %get-tuple-element.61.queries, bf16[1408,768]{1,0:T(8,128)(2,1)} %get-tuple-element.62.keys, ...), custom_call_target="tpu_custom_call" | custom-call | tf_op jit(solution)/shard_map/attend/pallas_call | solution.py:387
  55.9 38.3 %mlp.1 = (bf16[1024,768]{1,0:T(8,128)(2,1)}, bf16[1024,768]{1,0:T(8,128)(2,1)}, f32[1024,768]{1,0:T(8,128)}, bf16[5,192,384]{2,1,0:T(8,128)(2,1)}, bf16[5,192,38...) custom-call(bf16[1024,768]{1,0:T(8,128)(2,1)} %bitcast.8, ...), custom_call_target="tpu_custom_call" | custom-call | tf_op jit(solution)/shard_map/mlp/pallas_call | solution.py:954
  94.1 1.5 collective-permute-start
  95.6 1.6 collective-permute-start.1
  97.2 1.4 collective-permute-start.2
  98.6 42.8 %attend_back.1 = (bf16[1024,768]{1,0:T(8,128)(2,1)}, bf16[1152,768]{1,0:T(8,128)(2,1)}, bf16[1152,768]{1,0:T(8,128)(2,1)}) custom-call(s32[10]{0:T(128)} %get-tuple-element.71.meta, bf16[1024,768]{1,0:T(8,128)(2,1)} %get-tuple-element.72.sorted_queries, bf16[1408,768]{1,0:T(8,128)(2,1)} %get-tuple-element.62.keys, ...), custom_call_target="tpu_custom_call" | custom-call | tf_op jit(solution)/shard_map/attend_back/pallas_call | solution.py:417
  141.5 0.0 collective-permute-done.from_first
  141.5 0.0 copy-start.2
  141.5 0.0 collective-permute-done.1.from_second
  141.5 0.0 copy-start.3
  141.5 0.0 collective-permute-done.2.from_both
  141.5 0.0 copy-start.4
  141.5 0.8 copy-done.2
  142.3 0.2 copy-done.3
  142.6 0.2 copy-done.4
  142.8 84.5 %reduce.1 = (bf16[1024,768]{1,0:T(8,128)(2,1)}, bf16[288,768]{1,0:T(8,128)(2,1)}, bf16[2,8,2,2,2,2,48,384]{7,6,5,4,3,2,1,0:T(8,128)(2,1)}, f32[16,768]{1,0:T(8,128)}) custom-call(bf16[5,192,384]{2,1,0:T(8,128)(2,1)} %get-tuple-element.66.kept, bf16[5,192,384]{2,1,0:T(8,128)(2,1)} %copy-done.2, bf16[5,192,384]{2,1,0:T(8,128)(2,1)} %copy-done.3, ...), custom_call_target="tpu_custom_call" | custom-call | tf_op jit(solution)/shard_map/reduce/pallas_call | solution.py:996
  227.4 0.0 copy-start
  227.4 12.2 %widen.1 = (f32[1536,768]{1,0:T(8,128)}, f32[768,1536]{1,0:T(8,128)}, f32[768,768]{1,0:T(8,128)}, f32[768,768]{1,0:T(8,128)}, f32[768,768]{1,0:T(8,128)}, /*inde...) custom-call(bf16[2,6144,384]{2,1,0:T(8,128)(2,1)} %bitcast.10, ...), custom_call_target="tpu_custom_call" | custom-call | tf_op jit(solution)/shard_map/widen/pallas_call | solution.py:1036
  239.6 0.0 copy-done
  239.6 0.0 copy-start.1
  239.6 1.1 copy.42
  240.8 0.8 copy-done.1
  241.6 0.0 copy-start.5
  241.6 1.1 copy.43
  242.7 0.2 copy-done.5
  242.9 0.8 copy.44
Async XLA Ops:
  94.1 47.3 %collective-permute-start = (bf16[5,192,384]{2,1,0:T(8,128)(2,1)}, bf16[5,192,384]{2,1,0:T(8,128)(2,1)S(1)}, u32[]{:S(2)}, u32[]{:S(2)}) collective-permute-start(bf16[5,192,384]{2,1,0:T(8,128)(2,1)} %get-tuple-element.67), channel_id=1, source_target_pairs={{0,4},{1,5},{2,6},{3,7},{4,0},{5,1},{6,2},{7,3},{8,12},{9,13},{10,... | collective-permute-start | bytes 2211848 | tf_op jit(solution)/shard_map/ppermute | solution.py:983
  95.6 45.8 %collective-permute-start.1 = (bf16[5,192,384]{2,1,0:T(8,128)(2,1)}, bf16[5,192,384]{2,1,0:T(8,128)(2,1)S(1)}, u32[]{:S(2)}, u32[]{:S(2)}) collective-permute-start(bf16[5,192,384]{2,1,0:T(8,128)(2,1)} %get-tuple-element.68), channel_id=1, source_target_pairs={{0,2},{1,3},{2,0},{3,1},{4,6},{5,7},{6,4},{7,5},{8,10},{9,11},{10,... | collective-permute-start | bytes 2211848 | tf_op jit(solution)/shard_map/ppermute | solution.py:983
  97.2 44.2 %collective-permute-start.2 = (bf16[5,192,384]{2,1,0:T(8,128)(2,1)}, bf16[5,192,384]{2,1,0:T(8,128)(2,1)S(1)}, u32[]{:S(2)}, u32[]{:S(2)}) collective-permute-start(bf16[5,192,384]{2,1,0:T(8,128)(2,1)} %get-tuple-element.69), channel_id=1, source_target_pairs={{0,6},{1,7},{2,4},{3,5},{4,2},{5,3},{6,0},{7,1},{8,14},{9,15},{10,... | collective-permute-start | bytes 2211848 | tf_op jit(solution)/shard_map/ppermute | solution.py:983
  141.5 0.9 copy-start.2
  141.5 1.1 copy-start.3
  141.5 1.3 copy-start.4
  227.4 12.2 %copy-start = (bf16[1024,768]{1,0:T(8,128)(2,1)S(1)}, bf16[1024,768]{1,0:T(8,128)(2,1)}, u32[]{:S(2)}) copy-start(bf16[1024,768]{1,0:T(8,128)(2,1)} %get-tuple-element.65) | copy-start | bytes 4718596
  239.6 2.0 copy-start.1
  241.6 1.3 copy-start.5
